TPU v7x, 32 devices: a whole 2x2x4 slice. The times are simulated.
32 devices in a mesh: dp: 2 (over x), ctx: 16 (over z, y, core).
Axes of the slice: x: 2, y: 2, z: 4, core: 2. Of those that a mesh axis runs over, the one named last changes fastest.
Arguments:
- tokens: bfloat16 [2, 2048, 1152], P('dp', 'ctx'), may hold values from -50 to 50
- cotangent: bfloat16 [2, 2048, 1152], P('dp', 'ctx'), may hold values from -45 to 45
- clip_frames: int32 [2, 8], P('dp'), may hold values from 1 to 8, as said below
- clip_offsets: int32 [2, 8], P('dp'), may hold values from 0 to 1920, as said below
- clip_heights: int32 [2, 8], P('dp'), may hold values from 8 to 16, as said below
- clip_widths: int32 [2, 8], P('dp'), may hold values from 4 to 8
- spatial_gain: float32 [1152], replicated, may hold values from 0.1 to 1.9
- spatial_qkv: bfloat16 [1728, 1152], P('ctx'), may hold values from -0.1875 to 0.1875
- spatial_out: bfloat16 [576, 1152], P('ctx'), may hold values from -0.25 to 0.25
- temporal_gain: float32 [1152], replicated, may hold values from 0.1 to 1.9
- temporal_qkv: bfloat16 [1728, 1152], P('ctx'), may hold values from -0.1875 to 0.1875
- temporal_out: bfloat16 [576, 1152], P('ctx'), may hold values from -0.25 to 0.25
Outputs:
- output: bfloat16 [2, 2048, 1152], P('dp', 'ctx')
- tokens_grad: bfloat16 [2, 2048, 1152], P('dp', 'ctx')
- gain_grads: float32 [2, 1152], replicated
Inputs may be any that keep to these rules, and one draw needn't show every extreme that they name: `clip_frames`: clip 0 of every bin starts at offset 0 and has exactly 8 frame tiles; every later clip starts after the one before it ends, and the last ends by tile 16. `clip_offsets`: offsets are multiples of 128 and rise from clip to clip; the last clip of every bin starts at tile 16 - 1. `clip_heights`: clip 0 of every bin has 16 rows and 8 columns; heights times widths never exceed 128.
All inputs are finite; a program needn't handle non-finite values.
Results may differ from a plain program's by a relative error of at most 0.024.
Values may be sent and summed in bfloat16 or wider, within the bound.
No kernel may reach another device: no remote copies, remote signals or barrier semaphores. Data moves between devices by JAX's collectives and lax.ppermute only.
A program may use at most 64 MiB of HBM per device.

v0:
```python
import functools
import math

import jax
import jax.numpy as jnp
from jax import lax
from jax.experimental import pallas as pl
from jax.experimental.pallas import tpu as pltpu
from jax.sharding import PartitionSpec as P

HEADS = 8
FRAME = 128
EPSILON = 1e-06
ROPE_BASE = 10000.0
F32 = jnp.float32
BF16 = jnp.bfloat16
VMEM_LIMIT = 12 * 1024 * 1024


def nn(a, b):
    return lax.dot_general(a, b, (((1,), (0,)), ((), ())), preferred_element_type=F32)


def nt(a, b):
    return lax.dot_general(a, b, (((1,), (1,)), ((), ())), preferred_element_type=F32)


def tn(a, b):
    return lax.dot_general(a, b, (((0,), (0,)), ((), ())), preferred_element_type=F32)


class Rows:
    def __init__(self, qkv_rows, out_rows, size):
        self.qkv, self.out = qkv_rows, out_rows
        self.shard = qkv_rows + out_rows
        self.total = self.shard * size
        self.inner = out_rows * size
        self.head = self.inner // HEADS
        cut = self.shard % 16 == 0
        self.qkv_cut = -(-qkv_rows // 16) * 16 if cut else self.shard
        self.out_cut = qkv_rows // 16 * 16 if cut else 0
        self.qkv_total = self.qkv_cut * size
        self.out_total = (self.shard - self.out_cut) * size

    def spans(self, first, count, per_shard, stride, shift):
        found = []
        row = first
        while row < first + count:
            block, inside = divmod(row, per_shard)
            length = min(per_shard - inside, first + count - row)
            place = block * stride + shift + inside
            if found and found[-1][0] + found[-1][1] == place:
                found[-1] = (found[-1][0], found[-1][1] + length)
            else:
                found.append((place, length))
            row += length
        return found

    def qkv_spans(self, which, head, stride):
        return self.spans(which * self.inner + head * self.head, self.head, self.qkv, stride, 0)

    def out_spans(self, head, cut):
        stride = self.shard - cut
        return self.spans(head * self.head, self.head, self.out, stride, self.qkv - cut)

    def qkv_weight(self, ref):
        if self.qkv_cut == self.shard:
            return ref[...].reshape(self.total, -1)
        return ref[:, : self.qkv_cut, :].reshape(self.qkv_total, -1)

    def out_weight(self, ref):
        if self.out_cut == 0:
            return ref[...].reshape(self.total, -1)
        return ref[:, self.out_cut :, :].reshape(self.out_total, -1)


def read_rows(ref, spans):
    parts = [ref[place : place + length, :] for place, length in spans]
    return parts[0] if len(parts) == 1 else jnp.concatenate(parts, axis=0)


def write_rows(ref, spans, value):
    done = 0
    for place, length in spans:
        ref[place : place + length, :] = value[done : done + length, :]
        done += length


def inverse_size(values):
    return lax.rsqrt(jnp.mean(values * values, axis=-1, keepdims=True) + EPSILON)


def norm_back(values, inverse, gain, grad):
    scaled = grad * gain
    middle = jnp.mean(scaled * values, axis=-1, keepdims=True)
    grad_values = inverse * scaled - values * (inverse * inverse * inverse * middle)
    grad_gain = jnp.sum(grad * (values * inverse), axis=0, keepdims=True)
    return grad_values, grad_gain


def shares_of(queries, keys, allowed, live, scale):
    scores = tn(keys, queries) * scale
    weights = jnp.where(allowed, jnp.exp(jnp.where(allowed, scores, 0.0)), 0.0)
    totals = jnp.sum(weights, axis=0, keepdims=True) + (1.0 - live)
    return weights * (1.0 / totals)


def attend_back(queries, keys, values, shares, shares_low, grad, scale):
    grad_shares = tn(values, grad)
    middle = jnp.sum(shares * grad_shares, axis=0, keepdims=True)
    grad_scores = (shares * (grad_shares - middle) * scale).astype(BF16)
    return nn(keys, grad_scores), nt(queries, grad_scores), nt(grad, shares_low)


def clips_at(clips, frames):
    counts, times, numbers = (jnp.zeros_like(frames) for _ in range(3))
    for clip in range(clips.shape[1]):
        start = clips[1, clip] // FRAME
        member = (frames >= start) & (frames < start + clips[0, clip])
        counts = jnp.where(member, clips[2, clip] * clips[3, clip], counts)
        times = jnp.where(member, frames - start, times)
        numbers = jnp.where(member, clip + 1, numbers)
    return counts, times, numbers


def ids(shape, dim):
    return lax.broadcasted_iota(jnp.int32, shape, dim)


def space_masks(clips):
    count = clips_at(clips, lax.axis_index("ctx").astype(jnp.int32))[0]
    return ids((FRAME, FRAME), 0) < count, (ids((1, FRAME), 1) < count).astype(F32)


def time_masks(clips, near, slots):
    rank = lax.axis_index("ctx")
    token = ids((1, FRAME), 1)
    slot = lax.rem(token, slots)
    counts, times, numbers = clips_at(clips, (rank // near) * near + token // slots)
    alive = lax.rem(rank, near) * slots + slot < counts
    group = (numbers * FRAME + slot).astype(F32)
    keys = jnp.where(alive, group, -1.0)
    allowed = jnp.broadcast_to(keys, (FRAME, FRAME)).T == group
    return allowed, alive.astype(F32), times.astype(F32)


def turn_tables(times, half):
    pair = ids((2 * half, FRAME), 0)
    lower = pair < half
    frequency = jnp.exp(jnp.where(lower, pair, pair - half).astype(F32) * (-math.log(ROPE_BASE) / half))
    angles = frequency * times
    sine = jnp.sin(angles)
    return jnp.cos(angles), jnp.where(lower, -sine, sine)


def out_columns(rows):
    return lax.rem(ids((1, rows.total), 1), rows.shard) >= rows.qkv


def weight_copies(layout, order, pieces, target, sems, which):
    count = target.shape[1]
    return [
        pltpu.make_async_copy(
            pieces[piece].at[pl.ds(first, count)], target.at[order[index]], sems.at[which, index]
        )
        for index, (piece, first) in enumerate(layout)
    ]


def gate(*arrays):
    anywhere = pl.BlockSpec(memory_space=pl.ANY)
    count = len(arrays)
    return pl.pallas_call(
        lambda *refs: None,
        out_shape=tuple(jax.ShapeDtypeStruct(array.shape, array.dtype) for array in arrays),
        in_specs=[anywhere] * count,
        out_specs=(anywhere,) * count,
        input_output_aliases={index: index for index in range(count)},
    )(*arrays)


def start_weights(layouts, order, pieces, space, time, sems):
    def start(first, second):
        for copy in weight_copies(first, order, pieces, space, sems, 0):
            copy.start()
        for copy in weight_copies(second, order, pieces, time, sems, 1):
            copy.start()

    plane = order[len(layouts[0])]

    @pl.when(plane == 0)
    def _():
        start(layouts[0], layouts[1])

    @pl.when(plane != 0)
    def _():
        start(layouts[1], layouts[0])


def wait_weights(layouts, order, pieces, target, sems, which):
    for copy in weight_copies(layouts[0], order, pieces, target, sems, which):
        copy.wait()


def front(rows, layouts, order_of, clips, tokens, gains, *refs):
    pieces, refs = refs[:-9], refs[-9:]
    hidden, saved, shares_out, sent, space, time, project, mixed, sems = refs
    order = order_of()
    start_weights(layouts, order, pieces, space, time, sems)
    allowed, live = space_masks(clips)
    values = tokens[0].astype(F32)
    normed = (values * inverse_size(values) * gains[:1]).astype(BF16)
    mixed[...] = jnp.zeros_like(mixed)
    stride = rows.qkv_cut
    length = stride if len(layouts[0]) > 1 else rows.total

    def project_from(layout):
        for index, (piece, first) in enumerate(layout):
            target = pl.ds(pl.multiple_of(order[index] * length, 16), length)
            project[target, :] = nt(pieces[piece][first : first + length, :], normed)

    pl.when(order[-1] == 0)(lambda: project_from(layouts[0]))
    pl.when(order[-1] != 0)(lambda: project_from(layouts[1]))
    saved[...] = project[...].astype(BF16)
    scale = rows.head ** (-0.5)
    for head in range(HEADS):
        query, key, value = (
            read_rows(project, rows.qkv_spans(which, head, stride)).astype(BF16) for which in range(3)
        )
        shares = shares_of(query, key, allowed, live, scale).astype(BF16)
        shares_out[head] = shares
        write_rows(mixed, rows.out_spans(head, rows.out_cut), nn(value, shares) * live)
    wait_weights(layouts, order, pieces, space, sems, 0)
    update = tn(mixed[...].astype(BF16), rows.out_weight(space))
    low = (values + update).astype(BF16)
    hidden[...] = low
    values = low.astype(F32)
    normed = (values * inverse_size(values) * gains[1:]).astype(BF16)
    wait_weights(layouts, order, pieces, time, sems, 1)
    both = nt(jnp.concatenate([normed, tokens[1]], axis=0), time[...].reshape(rows.total, -1))
    count = values.shape[0]
    sent[...] = jnp.where(out_columns(rows), both[count:], both[:count]).astype(BF16)


def time_core(rows, near, slots, clips, arrived, sent, project, result):
    allowed, live, times = time_masks(clips, near, slots)
    for first in range(0, rows.total, FRAME):
        project[first : first + FRAME, :] = arrived[:, first : first + FRAME].astype(F32).T
    scale = rows.head ** (-0.5)
    half = rows.head // 2
    cosine, sine = turn_tables(times, half)

    def swapped(vectors):
        return jnp.concatenate([vectors[half:], vectors[:half]], axis=0)

    for head in range(HEADS):
        turned = []
        for which in range(2):
            vectors = read_rows(project, rows.qkv_spans(which, head, rows.shard))
            turned.append((vectors * cosine + swapped(vectors) * sine).astype(BF16))
        query, key = turned
        value = read_rows(project, rows.qkv_spans(2, head, rows.shard)).astype(BF16)
        grad = (read_rows(project, rows.out_spans(head, 0)) * live).astype(BF16)
        shares = shares_of(query, key, allowed, live, scale)
        shares_low = shares.astype(BF16)
        write_rows(result, rows.out_spans(head, 0), nn(value, shares_low) * live)
        grads = attend_back(query, key, value, shares, shares_low, grad, scale)
        for which in range(2):
            turned_grad = grads[which].astype(BF16).astype(F32)
            write_rows(
                result,
                rows.qkv_spans(which, head, rows.shard),
                turned_grad * cosine - swapped(turned_grad) * sine,
            )
        write_rows(result, rows.qkv_spans(2, head, rows.shard), grads[2])
    for first in range(0, rows.total, FRAME):
        sent[:, first : first + FRAME] = result[first : first + FRAME, :].T.astype(BF16)


def finish(
    rows,
    clips,
    arrived,
    tokens,
    gains,
    time,
    space,
    hidden,
    saved,
    shares_in,
    output,
    grad_tokens,
    gain_parts,
    project,
    grad_project,
):
    count = arrived.shape[0]
    live = space_masks(clips)[1]
    received = arrived[...]
    zeros = jnp.zeros_like(received)
    mask = jnp.broadcast_to(out_columns(rows), received.shape)
    left = jnp.concatenate([jnp.where(mask, zeros, received), jnp.where(mask, received, zeros)], axis=0)
    both = nn(left, time[...].reshape(rows.total, -1))
    values = hidden[...].astype(F32)
    output[...] = (values + both[count:]).astype(BF16)
    grad_normed = both[:count].astype(BF16).astype(F32)
    grad_front, grad_time_gain = norm_back(values, inverse_size(values), gains[1:], grad_normed)
    grad_hidden = (tokens[1].astype(F32) + grad_front).astype(BF16)

    project[...] = nt(rows.out_weight(space), grad_hidden)
    grad_project[...] = jnp.zeros_like(grad_project)
    scale = rows.head ** (-0.5)
    for head in range(HEADS):
        spans = [rows.qkv_spans(which, head, rows.qkv_cut) for which in range(3)]
        query, key, value = (read_rows(saved, where).astype(BF16) for where in spans)
        grad = (read_rows(project, rows.out_spans(head, rows.out_cut)) * live).astype(BF16)
        shares_low = shares_in[head]
        grads = attend_back(query, key, value, shares_low.astype(F32), shares_low, grad, scale)
        for where, part in zip(spans, grads):
            write_rows(grad_project, where, part)
    grad_normed = tn(grad_project[...].astype(BF16), rows.qkv_weight(space)).astype(BF16).astype(F32)
    values = tokens[0].astype(F32)
    grad_values, grad_space_gain = norm_back(values, inverse_size(values), gains[:1], grad_normed)
    grad_tokens[...] = (grad_hidden.astype(F32) + grad_values).astype(BF16)
    both_gains = jnp.concatenate([grad_space_gain, grad_time_gain], axis=0).astype(gain_parts.dtype)
    gain_parts[...] = jnp.broadcast_to(both_gains[None], gain_parts.shape)


def call(body, out_shapes, scratch, clips, operands):
    whole = pl.BlockSpec(memory_space=pltpu.VMEM)
    scalars = pl.BlockSpec(memory_space=pltpu.SMEM)
    return pl.pallas_call(
        body,
        out_shape=out_shapes,
        in_specs=[scalars] + [whole] * len(operands),
        out_specs=jax.tree.map(lambda _: whole, out_shapes),
        scratch_shapes=scratch,
        compiler_params=pltpu.CompilerParams(vmem_limit_bytes=VMEM_LIMIT),
    )(clips, *operands)


def gather_ring(space_rows, time_rows, size, others):
    chips = size // 2
    chain = chips // 2
    shard = space_rows.shape[0]

    def chip_at(place):
        place = place % chips
        return 2 * place if place < chain else 2 * (chips - 1 - place) + 1

    ring_pairs = []
    for place in range(chips):
        ring_pairs.append((2 * chip_at(place), 2 * chip_at(place + 1)))
        ring_pairs.append((2 * chip_at(place) + 1, 2 * chip_at(place - 1) + 1))
    planes = lax.axis_size("dp")
    plane = lax.rem(lax.axis_index("dp"), 2)

    def ring(rows):
        return lax.ppermute(rows, "ctx", ring_pairs)

    def across(rows):
        return lax.ppermute(rows, "dp", [(index, index ^ 1) for index in range(planes)])

    def twin(rows):
        return lax.ppermute(rows, "ctx", [(index, index ^ 1) for index in range(size)])

    own = jnp.where(plane == 0, space_rows, time_rows)
    own_other = jnp.where(plane == 0, time_rows, space_rows)
    t0 = twin(own)
    t1 = ring(t0)
    o1 = ring(own)
    o2 = ring(o1)
    t0_other = twin(own_other)
    x_o1 = across(o1)
    t2 = ring(t1)
    o3 = ring(o2)
    o1_twin = twin(o1)
    t1_twin = twin(t1)
    t2, t1_twin, t0_other, o1_twin, *others = gate(t2, t1_twin, t0_other, o1_twin, *others)
    x_t1 = across(t1)
    o2_twin = twin(o2)
    t3 = ring(t2)
    t2_twin = twin(t2)
    x_o1_twin = twin(x_o1)
    o3_twin = twin(o3)
    x_o3 = across(o3)
    x_t1_twin = twin(x_t1)
    x_o2 = ring(x_o1)
    o4 = ring(o3)
    t3_twin = twin(t3)
    x_o4 = across(o4)
    x_t2 = ring(x_t1)
    o4_twin = twin(o4)
    x_t3 = ring(x_t2)
    x_o2_twin = twin(x_o2)
    x_o3_twin = twin(x_o3)
    x_t2_twin = twin(x_t2)
    x_o4_twin = twin(x_o4)
    x_t3_twin = twin(x_t3)
    mine = {"o0": (own, 0), "t0": (t0, 0)}
    other = {"o0": (own_other, 0), "t0": (t0_other, 0)}
    mine |= {"o1": (o1, 0), "o1_twin": (o1_twin, 0)}
    other |= {"o1": (x_o1, 0), "o1_twin": (x_o1_twin, 0)}
    mine |= {"t1": (t1, 0), "t1_twin": (t1_twin, 0)}
    other |= {"t1": (x_t1, 0), "t1_twin": (x_t1_twin, 0)}
    mine |= {"o2": (o2, 0), "o2_twin": (o2_twin, 0)}
    other |= {"o2": (x_o2, 0), "o2_twin": (x_o2_twin, 0)}
    mine |= {"t2": (t2, 0), "t2_twin": (t2_twin, 0)}
    other |= {"t2": (x_t2, 0), "t2_twin": (x_t2_twin, 0)}
    mine |= {"o3": (o3, 0), "o3_twin": (o3_twin, 0)}
    other |= {"o3": (x_o3, 0), "o3_twin": (x_o3_twin, 0)}
    mine |= {"t3": (t3, 0), "t3_twin": (t3_twin, 0)}
    other |= {"t3": (x_t3, 0), "t3_twin": (x_t3_twin, 0)}
    mine |= {"o4": (o4, 0), "o4_twin": (o4_twin, 0)}
    other |= {"o4": (x_o4, 0), "o4_twin": (x_o4_twin, 0)}
    names = ["o0", "t0", "o1", "o2", "o3", "o4", "t1", "t2", "t3"]
    twins = names[2:]

    def order_of():
        rank = lax.axis_index("ctx")
        chip, core = rank // 2, lax.rem(rank, 2)
        column, level = lax.rem(chip, 2), chip // 2
        place = jnp.where(column == 0, level, chips - 1 - level)

        def came(carrier, name):
            steps, shard_core = int(name[1]), carrier if name[0] == "o" else 1 - carrier
            at = lax.rem(place + steps * (2 * carrier - 1) + chips, chips)
            return 2 * jnp.where(at < chain, 2 * at, 2 * (chips - 1 - at) + 1) + shard_core

        order = [came(core, name) for name in names] + [came(1 - core, name) for name in twins]
        return order + [lax.rem(lax.axis_index("dp"), 2)]

    pieces, layouts = [], ([], [])
    for half, found in enumerate((mine, other)):
        for name in names + [name + "_twin" for name in twins]:
            array, first = found[name]
            place_in = [index for index, piece in enumerate(pieces) if piece is array]
            if not place_in:
                place_in = [len(pieces)]
                pieces.append(array)
            layouts[half].append((place_in[0], first * shard))
    return pieces, layouts, order_of, others


def gather_weights(space_rows, time_rows, size, others):
    if size == 16 and lax.axis_size("dp") % 2 == 0:
        return gather_ring(space_rows, time_rows, size, others)
    shard, features = space_rows.shape
    gathered = lax.all_gather(jnp.concatenate([space_rows, time_rows], axis=0), "ctx", axis=0)
    gathered = gathered.reshape(size, 2, shard, features)
    halves = [gathered[:, half].reshape(size * shard, features) for half in range(2)]
    return halves, ([(0, 0)], [(1, 0)]), lambda: [0, 0], others


def shards(
    tokens,
    cotangent,
    clip_frames,
    clip_offsets,
    clip_heights,
    clip_widths,
    spatial_gain,
    spatial_qkv,
    spatial_out,
    temporal_gain,
    temporal_qkv,
    temporal_out,
):
    size = lax.axis_size("ctx")
    everyone = lax.axis_size("dp") * size
    count, features = tokens.shape[1], tokens.shape[2]
    assert count == FRAME and FRAME % size == 0
    near = size // 2
    slots = FRAME // near
    rows = Rows(spatial_qkv.shape[0], spatial_out.shape[0], size)
    both_tokens = jnp.concatenate([tokens, cotangent], axis=0)
    both_gains = jnp.stack([spatial_gain, temporal_gain])
    clips = jnp.concatenate([clip_frames, clip_offsets, clip_heights, clip_widths], axis=0)
    pieces, layouts, order_of, others = gather_weights(
        jnp.concatenate([spatial_qkv, spatial_out], axis=0),
        jnp.concatenate([temporal_qkv, temporal_out], axis=0),
        size,
        (both_tokens, both_gains, clips),
    )
    both_tokens, both_gains, clips = others
    wide = pltpu.VMEM((rows.total, FRAME), F32)
    qkv_wide = pltpu.VMEM((rows.qkv_total, FRAME), F32)
    out_wide = pltpu.VMEM((rows.out_total, FRAME), F32)
    blocks = len(layouts[0])
    sems = pltpu.SemaphoreType.DMA((2, blocks))
    weight_shape = jax.ShapeDtypeStruct((blocks, rows.total // blocks, features), BF16)
    groups = [list(range(first, first + near)) for first in range(0, size, near)]

    def exchange(sent):
        arrived = lax.all_to_all(
            sent.reshape(near, slots, rows.total),
            "ctx",
            split_axis=0,
            concat_axis=0,
            axis_index_groups=groups,
            tiled=True,
        )
        return arrived.reshape(FRAME, rows.total)

    hidden, saved, shares, sent, space_weights, time_weights = call(
        functools.partial(front, rows, layouts, order_of),
        (
            jax.ShapeDtypeStruct((FRAME, features), BF16),
            jax.ShapeDtypeStruct((rows.qkv_total, FRAME), BF16),
            jax.ShapeDtypeStruct((HEADS, FRAME, FRAME), BF16),
            jax.ShapeDtypeStruct((FRAME, rows.total), BF16),
            weight_shape,
            weight_shape,
        ),
        [qkv_wide, out_wide, sems],
        clips,
        (both_tokens, both_gains, *pieces),
    )
    arrived = exchange(sent)
    sent = call(
        functools.partial(time_core, rows, near, slots),
        jax.ShapeDtypeStruct((FRAME, rows.total), BF16),
        [wide, wide],
        clips,
        (arrived,),
    )
    arrived = exchange(sent)
    result, grad_tokens, gains = call(
        functools.partial(finish, rows),
        (
            jax.ShapeDtypeStruct((FRAME, features), BF16),
            jax.ShapeDtypeStruct((FRAME, features), BF16),
            jax.ShapeDtypeStruct((everyone, 2, features), BF16),
        ),
        [out_wide, qkv_wide],
        clips,
        (arrived, both_tokens, both_gains, time_weights, space_weights, hidden, saved, shares),
    )
    gains = lax.all_to_all(gains, ("dp", "ctx"), split_axis=0, concat_axis=0, tiled=True)
    gain_grads = jnp.sum(gains.astype(F32), axis=0) * (1.0 / math.sqrt(everyone * FRAME))
    return result[None], grad_tokens[None], gain_grads


def solution(mesh):
    return jax.shard_map(
        shards,
        mesh=mesh,
        in_specs=(
            P("dp", "ctx", None),
            P("dp", "ctx", None),
            P("dp", None),
            P("dp", None),
            P("dp", None),
            P("dp", None),
            P(),
            P("ctx", None),
            P("ctx", None),
            P(),
            P("ctx", None),
            P("ctx", None),
        ),
        out_specs=(P("dp", "ctx", None), P("dp", "ctx", None), P()),
        check_vma=False,
    )
```

profile of v0, /device:TPU:0, one launch (start us, length us, event | category | flops | bytes accessed | tf_op | source)
XLA Modules:
  0.0 127.6 jit_solution(16959672294080583414)
XLA Ops:
  0.6 1.3 %broadcast_select_fusion = (bf16[144,1152]{1,0:T(8,128)(2,1)S(1)}, bf16[144,1152]{1,0:T(8,128)(2,1)S(1)}) fusion(pred[]{:T(512)S(6)} %eq.4, bf16[36,1152]{1,0:T(8,128)(2,1)} %param.23, bf16[108,1152]{1,0:T(8,128)(2,1)} %param.22, bf16[36,1152]{1,0:T(8,128)(2,1)} %param.20, bf16[108,1152]{1,0:T(8,128)(2,1)} %param.19), kind=kLoop, calls=%fused_computation.3 | loop fusion | flops 1658880 | bytes 1327105 | tf_op jit(solution)/shard_map/jit(_where)/select_n | solution.py:368
  2.0 3.1 %collective-permute-start.5 = (bf16[144,1152]{1,0:T(8,128)(2,1)S(1)}, bf16[144,1152]{1,0:T(8,128)(2,1)S(1)}, u32[]{:S(2)}, u32[]{:S(2)}) collective-permute-start(bf16[144,1152]{1,0:T(8,128)(2,1)S(1)} %get-tuple-element.36.refs_0_), channel_id=1, source_target_pairs={{0,4},{1,3},{4,8},{5,1},{8,12},{9,5},{12,14},{13,9},{14,10},{15,13... | collective-permute-start | bytes 995336 | tf_op jit(solution)/shard_map/ppermute | solution.py:359
  5.0 5.0 %collective-permute-done.5.refs_2_ = bf16[144,1152]{1,0:T(8,128)(2,1)S(1)} collective-permute-done((bf16[144,1152]{1,0:T(8,128)(2,1)S(1)}, bf16[144,1152]{1,0:T(8,128)(2,1)S(1)}, u32[]{:S(2)}, u32[]{:S(2)}) %collective-permute-start.5) | collective-permute-done | bytes 331808 | tf_op jit(solution)/shard_map/ppermute | solution.py:359
  10.1 2.0 %collective-permute-start.16 = (bf16[144,1152]{1,0:T(8,128)(2,1)S(1)}, bf16[144,1152]{1,0:T(8,128)(2,1)S(1)}, u32[]{:S(2)}, u32[]{:S(2)}) collective-permute-start(bf16[144,1152]{1,0:T(8,128)(2,1)S(1)} %collective-permute-done.5.refs_2_), channel_id=1, source_target_pairs={{0,16},{16,0},{1,17},{17,1},{2,18},{18,2},{3,19},{19,3},{4,20},{20... | collective-permute-start | bytes 995336 | tf_op jit(solution)/shard_map/ppermute | solution.py:362
  12.1 1.6 %collective-permute-start.7 = (bf16[144,1152]{1,0:T(8,128)(2,1)S(1)}, bf16[144,1152]{1,0:T(8,128)(2,1)S(1)}, u32[]{:S(2)}, u32[]{:S(2)}) collective-permute-start(bf16[144,1152]{1,0:T(8,128)(2,1)S(1)} %collective-permute-done.5.refs_2_), channel_id=1, source_target_pairs={{0,4},{1,3},{4,8},{5,1},{8,12},{9,5},{12,14},{13,9},{14,10},{15,13... | collective-permute-start | bytes 995336 | tf_op jit(solution)/shard_map/ppermute | solution.py:359
  13.8 1.4 %collective-permute-start.1 = (bf16[144,1152]{1,0:T(8,128)(2,1)S(1)}, bf16[144,1152]{1,0:T(8,128)(2,1)S(1)}, u32[]{:S(2)}, u32[]{:S(2)}) collective-permute-start(bf16[144,1152]{1,0:T(8,128)(2,1)S(1)} %collective-permute-done.refs_1_), channel_id=1, source_target_pairs={{0,4},{1,3},{4,8},{5,1},{8,12},{9,5},{12,14},{13,9},{14,10},{15,13... | collective-permute-start | bytes 995336 | tf_op jit(solution)/shard_map/ppermute | solution.py:359
  15.2 3.9 %collective-permute-done.16.refs_18_ = bf16[144,1152]{1,0:T(8,128)(2,1)S(1)} collective-permute-done((bf16[144,1152]{1,0:T(8,128)(2,1)S(1)}, bf16[144,1152]{1,0:T(8,128)(2,1)S(1)}, u32[]{:S(2)}, u32[]{:S(2)}) %collective-permute-start.16) | collective-permute-done | bytes 331808 | tf_op jit(solution)/shard_map/ppermute | solution.py:362
  19.1 1.8 %collective-permute-start.17 = (bf16[144,1152]{1,0:T(8,128)(2,1)S(1)}, bf16[144,1152]{1,0:T(8,128)(2,1)S(1)}, u32[]{:S(2)}, u32[]{:S(2)}) collective-permute-start(bf16[144,1152]{1,0:T(8,128)(2,1)S(1)} %collective-permute-done.16.refs_18_), channel_id=1, source_target_pairs={{0,4},{1,3},{4,8},{5,1},{8,12},{9,5},{12,14},{13,9},{14,10},{15,13... | collective-permute-start | bytes 995336 | tf_op jit(solution)/shard_map/ppermute | solution.py:359
  21.0 1.5 %collective-permute-start.8 = (bf16[144,1152]{1,0:T(8,128)(2,1)S(1)}, bf16[144,1152]{1,0:T(8,128)(2,1)}, u32[]{:S(2)}, u32[]{:S(2)}) collective-permute-start(bf16[144,1152]{1,0:T(8,128)(2,1)S(1)} %collective-permute-done.7.refs_3_), channel_id=1, source_target_pairs={{0,4},{1,3},{4,8},{5,1},{8,12},{9,5},{12,14},{13,9},{14,10},{15,13... | collective-permute-start | bytes 995336 | tf_op jit(solution)/shard_map/ppermute | solution.py:359
  22.7 1.3 %collective-permute-start.20 = (bf16[144,1152]{1,0:T(8,128)(2,1)S(1)}, bf16[144,1152]{1,0:T(8,128)(2,1)}, u32[]{:S(2)}, u32[]{:S(2)}) collective-permute-start(bf16[144,1152]{1,0:T(8,128)(2,1)S(1)} %collective-permute-done.1.refs_6_), channel_id=1, source_target_pairs={{0,16},{16,0},{1,17},{17,1},{2,18},{18,2},{3,19},{19,3},{4,20},{20... | collective-permute-start | bytes 995336 | tf_op jit(solution)/shard_map/ppermute | solution.py:362
  24.8 1.5 %collective-permute-done.17.refs_19_ = bf16[144,1152]{1,0:T(8,128)(2,1)S(1)} collective-permute-done((bf16[144,1152]{1,0:T(8,128)(2,1)S(1)}, bf16[144,1152]{1,0:T(8,128)(2,1)S(1)}, u32[]{:S(2)}, u32[]{:S(2)}) %collective-permute-start.17) | collective-permute-done | bytes 331808 | tf_op jit(solution)/shard_map/ppermute | solution.py:359
  26.3 1.7 %collective-permute-start.2 = (bf16[144,1152]{1,0:T(8,128)(2,1)S(1)}, bf16[144,1152]{1,0:T(8,128)(2,1)S(1)}, u32[]{:S(2)}, u32[]{:S(2)}) collective-permute-start(bf16[144,1152]{1,0:T(8,128)(2,1)S(1)} %collective-permute-done.1.refs_6_), channel_id=1, source_target_pairs={{0,4},{1,3},{4,8},{5,1},{8,12},{9,5},{12,14},{13,9},{14,10},{15,13... | collective-permute-start | bytes 995336 | tf_op jit(solution)/shard_map/ppermute | solution.py:359
  32.2 1.5 %collective-permute-start.18 = (bf16[144,1152]{1,0:T(8,128)(2,1)}, bf16[144,1152]{1,0:T(8,128)(2,1)}, u32[]{:S(2)}, u32[]{:S(2)}) collective-permute-start(bf16[144,1152]{1,0:T(8,128)(2,1)} %collective-permute-done.8.refs_4_), channel_id=1, source_target_pairs={{0,16},{16,0},{1,17},{17,1},{2,18},{18,2},{3,19},{19,3},{4,20},{20... | collective-permute-start | bytes 995336 | tf_op jit(solution)/shard_map/ppermute | solution.py:362
  34.0 1.6 %collective-permute-start.9 = (bf16[144,1152]{1,0:T(8,128)(2,1)}, bf16[144,1152]{1,0:T(8,128)(2,1)}, u32[]{:S(2)}, u32[]{:S(2)}) collective-permute-start(bf16[144,1152]{1,0:T(8,128)(2,1)} %collective-permute-done.8.refs_4_), channel_id=1, source_target_pairs={{0,4},{1,3},{4,8},{5,1},{8,12},{9,5},{12,14},{13,9},{14,10},{15,13... | collective-permute-start | bytes 995336 | tf_op jit(solution)/shard_map/ppermute | solution.py:359
  36.3 1.6 %collective-permute-start.21 = (bf16[144,1152]{1,0:T(8,128)(2,1)}, bf16[144,1152]{1,0:T(8,128)(2,1)}, u32[]{:S(2)}, u32[]{:S(2)}) collective-permute-start(bf16[144,1152]{1,0:T(8,128)(2,1)} %collective-permute-done.20.refs_22_), channel_id=1, source_target_pairs={{0,4},{1,3},{4,8},{5,1},{8,12},{9,5},{12,14},{13,9},{14,10},{15,13... | collective-permute-start | bytes 995336 | tf_op jit(solution)/shard_map/ppermute | solution.py:359
  37.9 1.3 %pad_add_fusion.refs_6_ = s32[4,8]{1,0:T(4,128)} fusion(s32[1,8]{1,0:T(1,128)} %param.17, s32[1,8]{1,0:T(1,128)} %param.16, s32[1,8]{1,0:T(1,128)} %param.15, s32[1,8]{1,0:T(1,128)} %param.14), kind=kLoop, calls=%fused_computation.8 | loop fusion | flops 96 | bytes 256 | tf_op jit(solution)/shard_map/concatenate | solution.py:478
  39.2 1.9 %pad_maximum_fusion.refs_4_ = bf16[2,128,1152]{2,1,0:T(8,128)(2,1)} fusion(bf16[1,128,1152]{2,1,0:T(8,128)(2,1)} %param.13, bf16[1,128,1152]{2,1,0:T(8,128)(2,1)} %param.12), kind=kLoop, calls=%fused_computation | loop fusion | flops 294912 | bytes 1179648 | tf_op jit(solution)/shard_map/concatenate | solution.py:476
  41.2 1.6 %collective-permute-done.18.refs_20_ = bf16[144,1152]{1,0:T(8,128)(2,1)} collective-permute-done((bf16[144,1152]{1,0:T(8,128)(2,1)}, bf16[144,1152]{1,0:T(8,128)(2,1)}, u32[]{:S(2)}, u32[]{:S(2)}) %collective-permute-start.18) | collective-permute-done | bytes 331808 | tf_op jit(solution)/shard_map/ppermute | solution.py:362
  42.8 1.6 %collective-permute-start.10 = (bf16[144,1152]{1,0:T(8,128)(2,1)}, bf16[144,1152]{1,0:T(8,128)(2,1)S(1)}, u32[]{:S(2)}, u32[]{:S(2)}) collective-permute-start(bf16[144,1152]{1,0:T(8,128)(2,1)} %get-tuple-element.22.refs_7_), channel_id=1, source_target_pairs={{0,4},{1,3},{4,8},{5,1},{8,12},{9,5},{12,14},{13,9},{14,10},{15,13... | collective-permute-start | bytes 995336 | tf_op jit(solution)/shard_map/ppermute | solution.py:359
  44.4 1.6 %collective-permute-start.19 = (bf16[144,1152]{1,0:T(8,128)(2,1)}, bf16[144,1152]{1,0:T(8,128)(2,1)S(1)}, u32[]{:S(2)}, u32[]{:S(2)}) collective-permute-start(bf16[144,1152]{1,0:T(8,128)(2,1)} %collective-permute-done.9.refs_5_), channel_id=1, source_target_pairs={{0,16},{16,0},{1,17},{17,1},{2,18},{18,2},{3,19},{19,3},{4,20},{20... | collective-permute-start | bytes 995336 | tf_op jit(solution)/shard_map/ppermute | solution.py:362
  45.9 1.6 %collective-permute-start.22 = (bf16[144,1152]{1,0:T(8,128)(2,1)}, bf16[144,1152]{1,0:T(8,128)(2,1)S(1)}, u32[]{:S(2)}, u32[]{:S(2)}) collective-permute-start(bf16[144,1152]{1,0:T(8,128)(2,1)} %collective-permute-done.21.refs_23_), channel_id=1, source_target_pairs={{0,4},{1,3},{4,8},{5,1},{8,12},{9,5},{12,14},{13,9},{14,10},{15,13... | collective-permute-start | bytes 995336 | tf_op jit(solution)/shard_map/ppermute | solution.py:359
  47.5 2.6 %collective-permute-done.10.refs_8_ = bf16[144,1152]{1,0:T(8,128)(2,1)S(1)} collective-permute-done((bf16[144,1152]{1,0:T(8,128)(2,1)}, bf16[144,1152]{1,0:T(8,128)(2,1)S(1)}, u32[]{:S(2)}, u32[]{:S(2)}) %collective-permute-start.10) | collective-permute-done | bytes 331808 | tf_op jit(solution)/shard_map/ppermute | solution.py:359
  50.6 4.2 %collective-permute-done.19.refs_21_ = bf16[144,1152]{1,0:T(8,128)(2,1)S(1)} collective-permute-done((bf16[144,1152]{1,0:T(8,128)(2,1)}, bf16[144,1152]{1,0:T(8,128)(2,1)S(1)}, u32[]{:S(2)}, u32[]{:S(2)}) %collective-permute-start.19) | collective-permute-done | bytes 331808 | tf_op jit(solution)/shard_map/ppermute | solution.py:362
  55.3 1.1 collective-permute-done.26.refs_28_
  56.9 1.1 copy-done
  58.0 1.0 copy-done.3
  68.1 11.0 %shard_map.140 = (bf16[128,1152]{1,0:T(8,128)(2,1)S(1)}, bf16[1792,128]{1,0:T(8,128)(2,1)S(1)}, bf16[8,128,128]{2,1,0:T(8,128)(2,1)S(1)}, bf16[128,2304]{1,0:T(8...) custom-call(s32[4,8]{1,0:T(4,128)S(1)} %copy-done.21, ...), custom_call_target="tpu_custom_call" | custom-call | tf_op jit(solution)/shard_map/pallas_call | solution.py:332
  79.1 13.0 %all_to_all.15 = bf16[8,16,2304]{2,1,0:T(8,128)(2,1)S(1)} all-to-all(bf16[8,16,2304]{2,1,0:T(8,128)(2,1)S(1)} %bitcast.9), channel_id=1, replica_groups={{0,1,2,3,4,5,6,7},{8,9,10,11,12,13,14,15},{16,17,18,19,20,21,22,23},{24..., dimensions={0} | all-to-all | bytes 1179648 | tf_op jit(solution)/shard_map/all_to_all | solution.py:495
  92.1 3.1 %shard_map.141 = bf16[128,2304]{1,0:T(8,128)(2,1)S(1)} custom-call(s32[4,8]{1,0:T(4,128)S(1)} %copy-done.21, bf16[128,2304]{1,0:T(8,128)(2,1)S(1)} %bitcast.7), custom_call_target="tpu_custom_call" | custom-call | tf_op jit(solution)/shard_map/pallas_call | solution.py:332
  95.3 12.8 %all_to_all.16 = bf16[8,16,2304]{2,1,0:T(8,128)(2,1)S(1)} all-to-all(bf16[8,16,2304]{2,1,0:T(8,128)(2,1)S(1)} %bitcast.8), channel_id=1, replica_groups={{0,1,2,3,4,5,6,7},{8,9,10,11,12,13,14,15},{16,17,18,19,20,21,22,23},{24..., dimensions={0} | all-to-all | bytes 1179648 | tf_op jit(solution)/shard_map/all_to_all | solution.py:495
  108.0 6.9 %shard_map.142 = (bf16[128,1152]{1,0:T(8,128)(2,1)}, bf16[128,1152]{1,0:T(8,128)(2,1)}, bf16[32,2,1152]{2,1,0:T(2,128)(2,1)S(1)}) custom-call(s32[4,8]{1,0:T(4,128)S(1)} %copy-done.21, bf16[128,2304]{1,0:T(8,128)(2,1)S(1)} %bitcast.6, bf16[2,128,1152]{2,1,0:T(8,128)(2,1)S(1)} %copy-done.1, f32[2,1152]{1,0:T(2,128)S(1)} %copy-done.20, ...), custom_call_target="tpu_custom_call" | custom-call | tf_op jit(solution)/shard_map/pallas_call | solution.py:332
  114.9 12.0 %all_to_all.17 = bf16[32,2,1152]{2,1,0:T(2,128)(2,1)S(1)} all-to-all(bf16[32,2,1152]{2,1,0:T(2,128)(2,1)S(1)} %get-tuple-element.34), channel_id=1, replica_groups=mesh['dp'=2,'ctx'=16] {'dp','ctx'}, dimensions={0} | all-to-all | bytes 294912 | tf_op jit(solution)/shard_map/all_to_all | solution.py:539
  (87 shorter events, 17.9 us)
Async XLA Ops:
  2.0 8.1 %collective-permute-start.5 = (bf16[144,1152]{1,0:T(8,128)(2,1)S(1)}, bf16[144,1152]{1,0:T(8,128)(2,1)S(1)}, u32[]{:S(2)}, u32[]{:S(2)}) collective-permute-start(bf16[144,1152]{1,0:T(8,128)(2,1)S(1)} %get-tuple-element.36.refs_0_), channel_id=1, source_target_pairs={{0,4},{1,3},{4,8},{5,1},{8,12},{9,5},{12,14},{13,9},{14,10},{15,13... | collective-permute-start | bytes 995336 | tf_op jit(solution)/shard_map/ppermute | solution.py:359
  5.0 8.8 %collective-permute-start = (bf16[144,1152]{1,0:T(8,128)(2,1)S(1)}, bf16[144,1152]{1,0:T(8,128)(2,1)S(1)}, u32[]{:S(2)}, u32[]{:S(2)}) collective-permute-start(bf16[144,1152]{1,0:T(8,128)(2,1)S(1)} %get-tuple-element.36.refs_0_), channel_id=1, source_target_pairs={{0,1},{1,0},{2,3},{3,2},{4,5},{5,4},{6,7},{7,6},{8,9},{9,8},{10,11... | collective-permute-start | bytes 995336 | tf_op jit(solution)/shard_map/ppermute | solution.py:365
  10.1 9.0 %collective-permute-start.16 = (bf16[144,1152]{1,0:T(8,128)(2,1)S(1)}, bf16[144,1152]{1,0:T(8,128)(2,1)S(1)}, u32[]{:S(2)}, u32[]{:S(2)}) collective-permute-start(bf16[144,1152]{1,0:T(8,128)(2,1)S(1)} %collective-permute-done.5.refs_2_), channel_id=1, source_target_pairs={{0,16},{16,0},{1,17},{17,1},{2,18},{18,2},{3,19},{19,3},{4,20},{20... | collective-permute-start | bytes 995336 | tf_op jit(solution)/shard_map/ppermute | solution.py:362
  12.1 7.0 %collective-permute-start.4 = (bf16[144,1152]{1,0:T(8,128)(2,1)S(1)}, bf16[144,1152]{1,0:T(8,128)(2,1)S(1)}, u32[]{:S(2)}, u32[]{:S(2)}) collective-permute-start(bf16[144,1152]{1,0:T(8,128)(2,1)S(1)} %get-tuple-element.35.refs_16_), channel_id=1, source_target_pairs={{0,1},{1,0},{2,3},{3,2},{4,5},{5,4},{6,7},{7,6},{8,9},{9,8},{10,11... | collective-permute-start | bytes 995336 | tf_op jit(solution)/shard_map/ppermute | solution.py:365
  12.1 8.8 %collective-permute-start.7 = (bf16[144,1152]{1,0:T(8,128)(2,1)S(1)}, bf16[144,1152]{1,0:T(8,128)(2,1)S(1)}, u32[]{:S(2)}, u32[]{:S(2)}) collective-permute-start(bf16[144,1152]{1,0:T(8,128)(2,1)S(1)} %collective-permute-done.5.refs_2_), channel_id=1, source_target_pairs={{0,4},{1,3},{4,8},{5,1},{8,12},{9,5},{12,14},{13,9},{14,10},{15,13... | collective-permute-start | bytes 995336 | tf_op jit(solution)/shard_map/ppermute | solution.py:359
  13.6 7.4 %collective-permute-start.6 = (bf16[144,1152]{1,0:T(8,128)(2,1)S(1)}, bf16[144,1152]{1,0:T(8,128)(2,1)S(1)}, u32[]{:S(2)}, u32[]{:S(2)}) collective-permute-start(bf16[144,1152]{1,0:T(8,128)(2,1)S(1)} %collective-permute-done.5.refs_2_), channel_id=1, source_target_pairs={{0,1},{1,0},{2,3},{3,2},{4,5},{5,4},{6,7},{7,6},{8,9},{9,8},{10,11... | collective-permute-start | bytes 995336 | tf_op jit(solution)/shard_map/ppermute | solution.py:365
  13.8 8.9 %collective-permute-start.1 = (bf16[144,1152]{1,0:T(8,128)(2,1)S(1)}, bf16[144,1152]{1,0:T(8,128)(2,1)S(1)}, u32[]{:S(2)}, u32[]{:S(2)}) collective-permute-start(bf16[144,1152]{1,0:T(8,128)(2,1)S(1)} %collective-permute-done.refs_1_), channel_id=1, source_target_pairs={{0,4},{1,3},{4,8},{5,1},{8,12},{9,5},{12,14},{13,9},{14,10},{15,13... | collective-permute-start | bytes 995336 | tf_op jit(solution)/shard_map/ppermute | solution.py:359
  19.1 5.0 %collective-permute-start.23 = (bf16[144,1152]{1,0:T(8,128)(2,1)S(1)}, bf16[144,1152]{1,0:T(8,128)(2,1)S(1)}, u32[]{:S(2)}, u32[]{:S(2)}) collective-permute-start(bf16[144,1152]{1,0:T(8,128)(2,1)S(1)} %collective-permute-done.16.refs_18_), channel_id=1, source_target_pairs={{0,1},{1,0},{2,3},{3,2},{4,5},{5,4},{6,7},{7,6},{8,9},{9,8},{10,11... | collective-permute-start | bytes 995336 | tf_op jit(solution)/shard_map/ppermute | solution.py:365
  19.1 22.0 %copy-start.2 = (bf16[144,1152]{1,0:T(8,128)(2,1)}, bf16[144,1152]{1,0:T(8,128)(2,1)S(1)}, u32[]{:S(2)}) copy-start(bf16[144,1152]{1,0:T(8,128)(2,1)S(1)} %collective-permute-done.4.refs_2_) | copy-start | bytes 995332
  19.1 7.2 %collective-permute-start.17 = (bf16[144,1152]{1,0:T(8,128)(2,1)S(1)}, bf16[144,1152]{1,0:T(8,128)(2,1)S(1)}, u32[]{:S(2)}, u32[]{:S(2)}) collective-permute-start(bf16[144,1152]{1,0:T(8,128)(2,1)S(1)} %collective-permute-done.16.refs_18_), channel_id=1, source_target_pairs={{0,4},{1,3},{4,8},{5,1},{8,12},{9,5},{12,14},{13,9},{14,10},{15,13... | collective-permute-start | bytes 995336 | tf_op jit(solution)/shard_map/ppermute | solution.py:359
  20.9 7.9 %collective-permute-start.11 = (bf16[144,1152]{1,0:T(8,128)(2,1)S(1)}, bf16[144,1152]{1,0:T(8,128)(2,1)S(1)}, u32[]{:S(2)}, u32[]{:S(2)}) collective-permute-start(bf16[144,1152]{1,0:T(8,128)(2,1)S(1)} %collective-permute-done.7.refs_3_), channel_id=1, source_target_pairs={{0,1},{1,0},{2,3},{3,2},{4,5},{5,4},{6,7},{7,6},{8,9},{9,8},{10,11... | collective-permute-start | bytes 995336 | tf_op jit(solution)/shard_map/ppermute | solution.py:365
  21.0 11.2 %collective-permute-start.8 = (bf16[144,1152]{1,0:T(8,128)(2,1)S(1)}, bf16[144,1152]{1,0:T(8,128)(2,1)}, u32[]{:S(2)}, u32[]{:S(2)}) collective-permute-start(bf16[144,1152]{1,0:T(8,128)(2,1)S(1)} %collective-permute-done.7.refs_3_), channel_id=1, source_target_pairs={{0,4},{1,3},{4,8},{5,1},{8,12},{9,5},{12,14},{13,9},{14,10},{15,13... | collective-permute-start | bytes 995336 | tf_op jit(solution)/shard_map/ppermute | solution.py:359
  22.7 11.0 %collective-permute-start.20 = (bf16[144,1152]{1,0:T(8,128)(2,1)S(1)}, bf16[144,1152]{1,0:T(8,128)(2,1)}, u32[]{:S(2)}, u32[]{:S(2)}) collective-permute-start(bf16[144,1152]{1,0:T(8,128)(2,1)S(1)} %collective-permute-done.1.refs_6_), channel_id=1, source_target_pairs={{0,16},{16,0},{1,17},{17,1},{2,18},{18,2},{3,19},{19,3},{4,20},{20... | collective-permute-start | bytes 995336 | tf_op jit(solution)/shard_map/ppermute | solution.py:362
  24.8 9.2 %collective-permute-start.3 = (bf16[144,1152]{1,0:T(8,128)(2,1)S(1)}, bf16[144,1152]{1,0:T(8,128)(2,1)S(1)}, u32[]{:S(2)}, u32[]{:S(2)}) collective-permute-start(bf16[144,1152]{1,0:T(8,128)(2,1)S(1)} %collective-permute-done.1.refs_6_), channel_id=1, source_target_pairs={{0,1},{1,0},{2,3},{3,2},{4,5},{5,4},{6,7},{7,6},{8,9},{9,8},{10,11... | collective-permute-start | bytes 995336 | tf_op jit(solution)/shard_map/ppermute | solution.py:365
  26.3 9.3 %collective-permute-start.2 = (bf16[144,1152]{1,0:T(8,128)(2,1)S(1)}, bf16[144,1152]{1,0:T(8,128)(2,1)S(1)}, u32[]{:S(2)}, u32[]{:S(2)}) collective-permute-start(bf16[144,1152]{1,0:T(8,128)(2,1)S(1)} %collective-permute-done.1.refs_6_), channel_id=1, source_target_pairs={{0,4},{1,3},{4,8},{5,1},{8,12},{9,5},{12,14},{13,9},{14,10},{15,13... | collective-permute-start | bytes 995336 | tf_op jit(solution)/shard_map/ppermute | solution.py:359
  29.5 6.1 %collective-permute-start.24 = (bf16[144,1152]{1,0:T(8,128)(2,1)S(1)}, bf16[144,1152]{1,0:T(8,128)(2,1)S(1)}, u32[]{:S(2)}, u32[]{:S(2)}) collective-permute-start(bf16[144,1152]{1,0:T(8,128)(2,1)S(1)} %collective-permute-done.17.refs_19_), channel_id=1, source_target_pairs={{0,1},{1,0},{2,3},{3,2},{4,5},{5,4},{6,7},{7,6},{8,9},{9,8},{10,11... | collective-permute-start | bytes 995336 | tf_op jit(solution)/shard_map/ppermute | solution.py:365
  32.2 10.5 %collective-permute-start.18 = (bf16[144,1152]{1,0:T(8,128)(2,1)}, bf16[144,1152]{1,0:T(8,128)(2,1)}, u32[]{:S(2)}, u32[]{:S(2)}) collective-permute-start(bf16[144,1152]{1,0:T(8,128)(2,1)} %collective-permute-done.8.refs_4_), channel_id=1, source_target_pairs={{0,16},{16,0},{1,17},{17,1},{2,18},{18,2},{3,19},{19,3},{4,20},{20... | collective-permute-start | bytes 995336 | tf_op jit(solution)/shard_map/ppermute | solution.py:362
  33.7 9.0 %collective-permute-start.12 = (bf16[144,1152]{1,0:T(8,128)(2,1)}, bf16[144,1152]{1,0:T(8,128)(2,1)}, u32[]{:S(2)}, u32[]{:S(2)}) collective-permute-start(bf16[144,1152]{1,0:T(8,128)(2,1)} %collective-permute-done.8.refs_4_), channel_id=1, source_target_pairs={{0,1},{1,0},{2,3},{3,2},{4,5},{5,4},{6,7},{7,6},{8,9},{9,8},{10,11... | collective-permute-start | bytes 995336 | tf_op jit(solution)/shard_map/ppermute | solution.py:365
  34.0 10.4 %collective-permute-start.9 = (bf16[144,1152]{1,0:T(8,128)(2,1)}, bf16[144,1152]{1,0:T(8,128)(2,1)}, u32[]{:S(2)}, u32[]{:S(2)}) collective-permute-start(bf16[144,1152]{1,0:T(8,128)(2,1)} %collective-permute-done.8.refs_4_), channel_id=1, source_target_pairs={{0,4},{1,3},{4,8},{5,1},{8,12},{9,5},{12,14},{13,9},{14,10},{15,13... | collective-permute-start | bytes 995336 | tf_op jit(solution)/shard_map/ppermute | solution.py:359
  35.5 8.8 %collective-permute-start.27 = (bf16[144,1152]{1,0:T(8,128)(2,1)}, bf16[144,1152]{1,0:T(8,128)(2,1)}, u32[]{:S(2)}, u32[]{:S(2)}) collective-permute-start(bf16[144,1152]{1,0:T(8,128)(2,1)} %collective-permute-done.20.refs_22_), channel_id=1, source_target_pairs={{0,1},{1,0},{2,3},{3,2},{4,5},{5,4},{6,7},{7,6},{8,9},{9,8},{10,11... | collective-permute-start | bytes 995336 | tf_op jit(solution)/shard_map/ppermute | solution.py:365
  36.3 9.6 %collective-permute-start.21 = (bf16[144,1152]{1,0:T(8,128)(2,1)}, bf16[144,1152]{1,0:T(8,128)(2,1)}, u32[]{:S(2)}, u32[]{:S(2)}) collective-permute-start(bf16[144,1152]{1,0:T(8,128)(2,1)} %collective-permute-done.20.refs_22_), channel_id=1, source_target_pairs={{0,4},{1,3},{4,8},{5,1},{8,12},{9,5},{12,14},{13,9},{14,10},{15,13... | collective-permute-start | bytes 995336 | tf_op jit(solution)/shard_map/ppermute | solution.py:359
  42.8 4.7 %collective-permute-start.14 = (bf16[144,1152]{1,0:T(8,128)(2,1)}, bf16[144,1152]{1,0:T(8,128)(2,1)S(1)}, u32[]{:S(2)}, u32[]{:S(2)}) collective-permute-start(bf16[144,1152]{1,0:T(8,128)(2,1)} %get-tuple-element.22.refs_7_), channel_id=1, source_target_pairs={{0,1},{1,0},{2,3},{3,2},{4,5},{5,4},{6,7},{7,6},{8,9},{9,8},{10,11... | collective-permute-start | bytes 995336 | tf_op jit(solution)/shard_map/ppermute | solution.py:365
  42.8 7.3 %collective-permute-start.10 = (bf16[144,1152]{1,0:T(8,128)(2,1)}, bf16[144,1152]{1,0:T(8,128)(2,1)S(1)}, u32[]{:S(2)}, u32[]{:S(2)}) collective-permute-start(bf16[144,1152]{1,0:T(8,128)(2,1)} %get-tuple-element.22.refs_7_), channel_id=1, source_target_pairs={{0,4},{1,3},{4,8},{5,1},{8,12},{9,5},{12,14},{13,9},{14,10},{15,13... | collective-permute-start | bytes 995336 | tf_op jit(solution)/shard_map/ppermute | solution.py:359
  44.3 5.8 %collective-permute-start.25 = (bf16[144,1152]{1,0:T(8,128)(2,1)}, bf16[144,1152]{1,0:T(8,128)(2,1)S(1)}, u32[]{:S(2)}, u32[]{:S(2)}) collective-permute-start(bf16[144,1152]{1,0:T(8,128)(2,1)} %collective-permute-done.18.refs_20_), channel_id=1, source_target_pairs={{0,1},{1,0},{2,3},{3,2},{4,5},{5,4},{6,7},{7,6},{8,9},{9,8},{10,11... | collective-permute-start | bytes 995336 | tf_op jit(solution)/shard_map/ppermute | solution.py:365
  44.4 10.4 %collective-permute-start.19 = (bf16[144,1152]{1,0:T(8,128)(2,1)}, bf16[144,1152]{1,0:T(8,128)(2,1)S(1)}, u32[]{:S(2)}, u32[]{:S(2)}) collective-permute-start(bf16[144,1152]{1,0:T(8,128)(2,1)} %collective-permute-done.9.refs_5_), channel_id=1, source_target_pairs={{0,16},{16,0},{1,17},{17,1},{2,18},{18,2},{3,19},{19,3},{4,20},{20... | collective-permute-start | bytes 995336 | tf_op jit(solution)/shard_map/ppermute | solution.py:362
  45.9 8.9 %collective-permute-start.22 = (bf16[144,1152]{1,0:T(8,128)(2,1)}, bf16[144,1152]{1,0:T(8,128)(2,1)S(1)}, u32[]{:S(2)}, u32[]{:S(2)}) collective-permute-start(bf16[144,1152]{1,0:T(8,128)(2,1)} %collective-permute-done.21.refs_23_), channel_id=1, source_target_pairs={{0,4},{1,3},{4,8},{5,1},{8,12},{9,5},{12,14},{13,9},{14,10},{15,13... | collective-permute-start | bytes 995336 | tf_op jit(solution)/shard_map/ppermute | solution.py:359
  47.5 7.8 %collective-permute-start.13 = (bf16[144,1152]{1,0:T(8,128)(2,1)}, bf16[144,1152]{1,0:T(8,128)(2,1)S(1)}, u32[]{:S(2)}, u32[]{:S(2)}) collective-permute-start(bf16[144,1152]{1,0:T(8,128)(2,1)} %collective-permute-done.9.refs_5_), channel_id=1, source_target_pairs={{0,1},{1,0},{2,3},{3,2},{4,5},{5,4},{6,7},{7,6},{8,9},{9,8},{10,11... | collective-permute-start | bytes 995336 | tf_op jit(solution)/shard_map/ppermute | solution.py:365
  50.1 5.2 %collective-permute-start.28 = (bf16[144,1152]{1,0:T(8,128)(2,1)}, bf16[144,1152]{1,0:T(8,128)(2,1)S(1)}, u32[]{:S(2)}, u32[]{:S(2)}) collective-permute-start(bf16[144,1152]{1,0:T(8,128)(2,1)} %collective-permute-done.21.refs_23_), channel_id=1, source_target_pairs={{0,1},{1,0},{2,3},{3,2},{4,5},{5,4},{6,7},{7,6},{8,9},{9,8},{10,11... | collective-permute-start | bytes 995336 | tf_op jit(solution)/shard_map/ppermute | solution.py:365
  50.1 5.2 %collective-permute-start.15 = (bf16[144,1152]{1,0:T(8,128)(2,1)S(1)}, bf16[144,1152]{1,0:T(8,128)(2,1)S(1)}, u32[]{:S(2)}, u32[]{:S(2)}) collective-permute-start(bf16[144,1152]{1,0:T(8,128)(2,1)S(1)} %collective-permute-done.10.refs_8_), channel_id=1, source_target_pairs={{0,1},{1,0},{2,3},{3,2},{4,5},{5,4},{6,7},{7,6},{8,9},{9,8},{10,11... | collective-permute-start | bytes 995336 | tf_op jit(solution)/shard_map/ppermute | solution.py:365
  54.8 1.6 %collective-permute-start.26 = (bf16[144,1152]{1,0:T(8,128)(2,1)S(1)}, bf16[144,1152]{1,0:T(8,128)(2,1)S(1)}, u32[]{:S(2)}, u32[]{:S(2)}) collective-permute-start(bf16[144,1152]{1,0:T(8,128)(2,1)S(1)} %collective-permute-done.19.refs_21_), channel_id=1, source_target_pairs={{0,1},{1,0},{2,3},{3,2},{4,5},{5,4},{6,7},{7,6},{8,9},{9,8},{10,11... | collective-permute-start | bytes 995336 | tf_op jit(solution)/shard_map/ppermute | solution.py:365
  54.8 2.1 %collective-permute-start.29 = (bf16[144,1152]{1,0:T(8,128)(2,1)S(1)}, bf16[144,1152]{1,0:T(8,128)(2,1)S(1)}, u32[]{:S(2)}, u32[]{:S(2)}) collective-permute-start(bf16[144,1152]{1,0:T(8,128)(2,1)S(1)} %collective-permute-done.22.refs_24_), channel_id=1, source_target_pairs={{0,1},{1,0},{2,3},{3,2},{4,5},{5,4},{6,7},{7,6},{8,9},{9,8},{10,11... | collective-permute-start | bytes 995336 | tf_op jit(solution)/shard_map/ppermute | solution.py:365
  68.1 39.9 %copy-start.1 = (bf16[2,128,1152]{2,1,0:T(8,128)(2,1)S(1)}, bf16[2,128,1152]{2,1,0:T(8,128)(2,1)}, u32[]{:S(2)}) copy-start(bf16[2,128,1152]{2,1,0:T(8,128)(2,1)} %get-tuple-element.20.tokens) | copy-start | bytes 1769476
  (20 other events, 47.8 us)
where the time goes:
time: 128 us
  blocking collectives  37.8 us (30%)
  starting transfers between devices  25.3 us (20%)
  Pallas kernels  21 us (16%)
  waiting for transfers between devices  20.6 us (16%)
  local copies, waits for them, and re-layouts  16.3 us (13%)
  other arithmetic  5.89 us (5%)
    all_to_all x2, blocking collectives, exchange(): lax.all_to_all(sent.reshape(near, slots, rows.total), 'ctx', split_axis=0...  25.8 us
    pallas_call x3, Pallas kernels, call(): pl.pallas_call(body, out_shape=out_shapes, in_specs=[scalars] + [whole] *...  21 us
    ppermute x10, starting transfers between devices, ring(): return lax.ppermute(rows, 'ctx', ring_pairs)  17.4 us
    unnamed x44, local copies, waits for them, and re-layouts  14.9 us
    all_to_all x1, blocking collectives, shards(): lax.all_to_all(gains, ('dp', 'ctx'), split_axis=0, concat_axis=0, tiled=T...  12 us
    ppermute x4, waiting for transfers between devices, across(): lax.ppermute(rows, 'dp', [(index, index ^ 1) for index in range(planes)])  9.62 us
    ppermute x10, waiting for transfers between devices, ring(): return lax.ppermute(rows, 'ctx', ring_pairs)  9.35 us
    ppermute x4, starting transfers between devices, across(): lax.ppermute(rows, 'dp', [(index, index ^ 1) for index in range(planes)])  6.34 us
  transfers between devices with their start and end apart: 30, of which 9 were waited for; matrix products, arithmetic and copies ran while one was open for 4% of the time, Pallas kernels for 0%

commit v1 on v0

--- a/solution.py
+++ b/solution.py
@@ -176,6 +176,7 @@
         in_specs=[anywhere] * count,
         out_specs=(anywhere,) * count,
         input_output_aliases={index: index for index in range(count)},
+        compiler_params=pltpu.CompilerParams(vmem_limit_bytes=1024 * 1024),
     )(*arrays)
 
 

time: 128 us -> 112 us (0.88)
  local copies, waits for them, and re-layouts: 16.3 us -> 1.4 us
  waiting for transfers between devices: 20.6 us -> 23.3 us
  other arithmetic: 5.89 us -> 3.89 us
    unnamed x44 -> x0, local copies, waits for them, and re-layouts: 14.9 us -> none
    ppermute x4, waiting for transfers between devices: 9.62 us -> 11.2 us  [across(): lax.ppermute(rows, 'dp', [(index, index ^ 1) for index in range(planes)])]
  transfers between devices with their start and end apart: 30 -> 30, of which waited for: 9 -> 11; matrix products, arithmetic and copies ran while one was open for 4% -> 3% of each run, Pallas kernels for 0% -> 0%
where the time goes in v1:
time: 112 us
  blocking collectives  37.8 us (34%)
  starting transfers between devices  25 us (22%)
  waiting for transfers between devices  23.3 us (21%)
  Pallas kernels  19.9 us (18%)
  other arithmetic  3.89 us (3%)
  local copies, waits for them, and re-layouts  1.4 us (1%)
    all_to_all x2, blocking collectives, exchange(): lax.all_to_all(sent.reshape(near, slots, rows.total), 'ctx', split_axis=0...  26.1 us
    pallas_call x3, Pallas kernels, call(): pl.pallas_call(body, out_shape=out_shapes, in_specs=[scalars] + [whole] *...  19.9 us
    ppermute x10, starting transfers between devices, ring(): return lax.ppermute(rows, 'ctx', ring_pairs)  17.1 us
    all_to_all x1, blocking collectives, shards(): lax.all_to_all(gains, ('dp', 'ctx'), split_axis=0, concat_axis=0, tiled=T...  11.6 us
    ppermute x4, waiting for transfers between devices, across(): lax.ppermute(rows, 'dp', [(index, index ^ 1) for index in range(planes)])  11.2 us
    ppermute x10, waiting for transfers between devices, ring(): return lax.ppermute(rows, 'ctx', ring_pairs)  10.5 us
    ppermute x4, starting transfers between devices, across(): lax.ppermute(rows, 'dp', [(index, index ^ 1) for index in range(planes)])  6.36 us
  transfers between devices with their start and end apart: 30, of which 11 were waited for; matrix products, arithmetic and copies ran while one was open for 3% of the time, Pallas kernels for 0%

profile of v1, /device:TPU:0, one launch (start us, length us, event | category | flops | bytes accessed | tf_op | source)
XLA Modules:
  0.0 112.0 jit_solution(358186795257372128)
XLA Ops:
  0.6 1.3 %broadcast_select_fusion = (bf16[144,1152]{1,0:T(8,128)(2,1)S(1)}, bf16[144,1152]{1,0:T(8,128)(2,1)S(1)}) fusion(pred[]{:T(512)S(6)} %eq.4, bf16[36,1152]{1,0:T(8,128)(2,1)} %param.23, bf16[108,1152]{1,0:T(8,128)(2,1)} %param.22, bf16[36,1152]{1,0:T(8,128)(2,1)} %param.20, bf16[108,1152]{1,0:T(8,128)(2,1)} %param.19), kind=kLoop, calls=%fused_computation.3 | loop fusion | flops 1658880 | bytes 1327105 | tf_op jit(solution)/shard_map/jit(_where)/select_n | solution.py:369
  2.0 3.1 %collective-permute-start.5 = (bf16[144,1152]{1,0:T(8,128)(2,1)S(1)}, bf16[144,1152]{1,0:T(8,128)(2,1)S(1)}, u32[]{:S(2)}, u32[]{:S(2)}) collective-permute-start(bf16[144,1152]{1,0:T(8,128)(2,1)S(1)} %get-tuple-element.36.refs_0_), channel_id=1, source_target_pairs={{0,4},{1,3},{4,8},{5,1},{8,12},{9,5},{12,14},{13,9},{14,10},{15,13... | collective-permute-start | bytes 995336 | tf_op jit(solution)/shard_map/ppermute | solution.py:360
  5.0 5.0 %collective-permute-done.5.refs_2_ = bf16[144,1152]{1,0:T(8,128)(2,1)S(1)} collective-permute-done((bf16[144,1152]{1,0:T(8,128)(2,1)S(1)}, bf16[144,1152]{1,0:T(8,128)(2,1)S(1)}, u32[]{:S(2)}, u32[]{:S(2)}) %collective-permute-start.5) | collective-permute-done | bytes 331808 | tf_op jit(solution)/shard_map/ppermute | solution.py:360
  10.1 2.0 %collective-permute-start.16 = (bf16[144,1152]{1,0:T(8,128)(2,1)S(1)}, bf16[144,1152]{1,0:T(8,128)(2,1)S(1)}, u32[]{:S(2)}, u32[]{:S(2)}) collective-permute-start(bf16[144,1152]{1,0:T(8,128)(2,1)S(1)} %collective-permute-done.5.refs_2_), channel_id=1, source_target_pairs={{0,16},{16,0},{1,17},{17,1},{2,18},{18,2},{3,19},{19,3},{4,20},{20... | collective-permute-start | bytes 995336 | tf_op jit(solution)/shard_map/ppermute | solution.py:363
  12.1 1.6 %collective-permute-start.7 = (bf16[144,1152]{1,0:T(8,128)(2,1)S(1)}, bf16[144,1152]{1,0:T(8,128)(2,1)S(1)}, u32[]{:S(2)}, u32[]{:S(2)}) collective-permute-start(bf16[144,1152]{1,0:T(8,128)(2,1)S(1)} %collective-permute-done.5.refs_2_), channel_id=1, source_target_pairs={{0,4},{1,3},{4,8},{5,1},{8,12},{9,5},{12,14},{13,9},{14,10},{15,13... | collective-permute-start | bytes 995336 | tf_op jit(solution)/shard_map/ppermute | solution.py:360
  13.8 1.4 %collective-permute-start.1 = (bf16[144,1152]{1,0:T(8,128)(2,1)S(1)}, bf16[144,1152]{1,0:T(8,128)(2,1)S(1)}, u32[]{:S(2)}, u32[]{:S(2)}) collective-permute-start(bf16[144,1152]{1,0:T(8,128)(2,1)S(1)} %collective-permute-done.refs_1_), channel_id=1, source_target_pairs={{0,4},{1,3},{4,8},{5,1},{8,12},{9,5},{12,14},{13,9},{14,10},{15,13... | collective-permute-start | bytes 995336 | tf_op jit(solution)/shard_map/ppermute | solution.py:360
  15.2 3.9 %collective-permute-done.16.refs_18_ = bf16[144,1152]{1,0:T(8,128)(2,1)S(1)} collective-permute-done((bf16[144,1152]{1,0:T(8,128)(2,1)S(1)}, bf16[144,1152]{1,0:T(8,128)(2,1)S(1)}, u32[]{:S(2)}, u32[]{:S(2)}) %collective-permute-start.16) | collective-permute-done | bytes 331808 | tf_op jit(solution)/shard_map/ppermute | solution.py:363
  19.1 1.7 %collective-permute-start.17 = (bf16[144,1152]{1,0:T(8,128)(2,1)S(1)}, bf16[144,1152]{1,0:T(8,128)(2,1)S(1)}, u32[]{:S(2)}, u32[]{:S(2)}) collective-permute-start(bf16[144,1152]{1,0:T(8,128)(2,1)S(1)} %collective-permute-done.16.refs_18_), channel_id=1, source_target_pairs={{0,4},{1,3},{4,8},{5,1},{8,12},{9,5},{12,14},{13,9},{14,10},{15,13... | collective-permute-start | bytes 995336 | tf_op jit(solution)/shard_map/ppermute | solution.py:360
  21.0 1.5 %collective-permute-start.8 = (bf16[144,1152]{1,0:T(8,128)(2,1)S(1)}, bf16[144,1152]{1,0:T(8,128)(2,1)S(1)}, u32[]{:S(2)}, u32[]{:S(2)}) collective-permute-start(bf16[144,1152]{1,0:T(8,128)(2,1)S(1)} %collective-permute-done.7.refs_3_), channel_id=1, source_target_pairs={{0,4},{1,3},{4,8},{5,1},{8,12},{9,5},{12,14},{13,9},{14,10},{15,13... | collective-permute-start | bytes 995336 | tf_op jit(solution)/shard_map/ppermute | solution.py:360
  22.7 1.2 %collective-permute-start.20 = (bf16[144,1152]{1,0:T(8,128)(2,1)S(1)}, bf16[144,1152]{1,0:T(8,128)(2,1)S(1)}, u32[]{:S(2)}, u32[]{:S(2)}) collective-permute-start(bf16[144,1152]{1,0:T(8,128)(2,1)S(1)} %collective-permute-done.1.refs_6_), channel_id=1, source_target_pairs={{0,16},{16,0},{1,17},{17,1},{2,18},{18,2},{3,19},{19,3},{4,20},{20... | collective-permute-start | bytes 995336 | tf_op jit(solution)/shard_map/ppermute | solution.py:363
  24.0 2.3 %collective-permute-done.17.refs_19_ = bf16[144,1152]{1,0:T(8,128)(2,1)S(1)} collective-permute-done((bf16[144,1152]{1,0:T(8,128)(2,1)S(1)}, bf16[144,1152]{1,0:T(8,128)(2,1)S(1)}, u32[]{:S(2)}, u32[]{:S(2)}) %collective-permute-start.17) | collective-permute-done | bytes 331808 | tf_op jit(solution)/shard_map/ppermute | solution.py:360
  26.3 1.7 %collective-permute-start.2 = (bf16[144,1152]{1,0:T(8,128)(2,1)S(1)}, bf16[144,1152]{1,0:T(8,128)(2,1)S(1)}, u32[]{:S(2)}, u32[]{:S(2)}) collective-permute-start(bf16[144,1152]{1,0:T(8,128)(2,1)S(1)} %collective-permute-done.1.refs_6_), channel_id=1, source_target_pairs={{0,4},{1,3},{4,8},{5,1},{8,12},{9,5},{12,14},{13,9},{14,10},{15,13... | collective-permute-start | bytes 995336 | tf_op jit(solution)/shard_map/ppermute | solution.py:360
  28.0 0.7 stack.9
  28.7 0.7 stack.10
  29.8 1.6 %collective-permute-start.18 = (bf16[144,1152]{1,0:T(8,128)(2,1)S(1)}, bf16[144,1152]{1,0:T(8,128)(2,1)S(1)}, u32[]{:S(2)}, u32[]{:S(2)}) collective-permute-start(bf16[144,1152]{1,0:T(8,128)(2,1)S(1)} %collective-permute-done.8.refs_4_), channel_id=1, source_target_pairs={{0,16},{16,0},{1,17},{17,1},{2,18},{18,2},{3,19},{19,3},{4,20},{20... | collective-permute-start | bytes 995336 | tf_op jit(solution)/shard_map/ppermute | solution.py:363
  32.1 1.6 %collective-permute-start.9 = (bf16[144,1152]{1,0:T(8,128)(2,1)S(1)}, bf16[144,1152]{1,0:T(8,128)(2,1)S(1)}, u32[]{:S(2)}, u32[]{:S(2)}) collective-permute-start(bf16[144,1152]{1,0:T(8,128)(2,1)S(1)} %collective-permute-done.8.refs_4_), channel_id=1, source_target_pairs={{0,4},{1,3},{4,8},{5,1},{8,12},{9,5},{12,14},{13,9},{14,10},{15,13... | collective-permute-start | bytes 995336 | tf_op jit(solution)/shard_map/ppermute | solution.py:360
  33.9 1.4 %collective-permute-start.21 = (bf16[144,1152]{1,0:T(8,128)(2,1)S(1)}, bf16[144,1152]{1,0:T(8,128)(2,1)S(1)}, u32[]{:S(2)}, u32[]{:S(2)}) collective-permute-start(bf16[144,1152]{1,0:T(8,128)(2,1)S(1)} %collective-permute-done.20.refs_22_), channel_id=1, source_target_pairs={{0,4},{1,3},{4,8},{5,1},{8,12},{9,5},{12,14},{13,9},{14,10},{15,13... | collective-permute-start | bytes 995336 | tf_op jit(solution)/shard_map/ppermute | solution.py:360
  35.3 0.7 pad_add_fusion.refs_6_
  36.0 1.1 pad_maximum_fusion.refs_4_
  37.2 2.5 %collective-permute-done.18.refs_20_ = bf16[144,1152]{1,0:T(8,128)(2,1)S(1)} collective-permute-done((bf16[144,1152]{1,0:T(8,128)(2,1)S(1)}, bf16[144,1152]{1,0:T(8,128)(2,1)S(1)}, u32[]{:S(2)}, u32[]{:S(2)}) %collective-permute-start.18) | collective-permute-done | bytes 331808 | tf_op jit(solution)/shard_map/ppermute | solution.py:363
  39.7 1.6 %collective-permute-start.10 = (bf16[144,1152]{1,0:T(8,128)(2,1)S(1)}, bf16[144,1152]{1,0:T(8,128)(2,1)S(1)}, u32[]{:S(2)}, u32[]{:S(2)}) collective-permute-start(bf16[144,1152]{1,0:T(8,128)(2,1)S(1)} %get-tuple-element.22.refs_7_), channel_id=1, source_target_pairs={{0,4},{1,3},{4,8},{5,1},{8,12},{9,5},{12,14},{13,9},{14,10},{15,13... | collective-permute-start | bytes 995336 | tf_op jit(solution)/shard_map/ppermute | solution.py:360
  41.3 1.6 %collective-permute-start.19 = (bf16[144,1152]{1,0:T(8,128)(2,1)S(1)}, bf16[144,1152]{1,0:T(8,128)(2,1)S(1)}, u32[]{:S(2)}, u32[]{:S(2)}) collective-permute-start(bf16[144,1152]{1,0:T(8,128)(2,1)S(1)} %collective-permute-done.9.refs_5_), channel_id=1, source_target_pairs={{0,16},{16,0},{1,17},{17,1},{2,18},{18,2},{3,19},{19,3},{4,20},{20... | collective-permute-start | bytes 995336 | tf_op jit(solution)/shard_map/ppermute | solution.py:363
  42.8 1.6 %collective-permute-start.22 = (bf16[144,1152]{1,0:T(8,128)(2,1)S(1)}, bf16[144,1152]{1,0:T(8,128)(2,1)S(1)}, u32[]{:S(2)}, u32[]{:S(2)}) collective-permute-start(bf16[144,1152]{1,0:T(8,128)(2,1)S(1)} %collective-permute-done.21.refs_23_), channel_id=1, source_target_pairs={{0,4},{1,3},{4,8},{5,1},{8,12},{9,5},{12,14},{13,9},{14,10},{15,13... | collective-permute-start | bytes 995336 | tf_op jit(solution)/shard_map/ppermute | solution.py:360
  44.4 2.4 %collective-permute-done.10.refs_8_ = bf16[144,1152]{1,0:T(8,128)(2,1)S(1)} collective-permute-done((bf16[144,1152]{1,0:T(8,128)(2,1)S(1)}, bf16[144,1152]{1,0:T(8,128)(2,1)S(1)}, u32[]{:S(2)}, u32[]{:S(2)}) %collective-permute-start.10) | collective-permute-done | bytes 331808 | tf_op jit(solution)/shard_map/ppermute | solution.py:360
  47.3 4.2 %collective-permute-done.19.refs_21_ = bf16[144,1152]{1,0:T(8,128)(2,1)S(1)} collective-permute-done((bf16[144,1152]{1,0:T(8,128)(2,1)S(1)}, bf16[144,1152]{1,0:T(8,128)(2,1)S(1)}, u32[]{:S(2)}, u32[]{:S(2)}) %collective-permute-start.19) | collective-permute-done | bytes 331808 | tf_op jit(solution)/shard_map/ppermute | solution.py:363
  52.0 1.1 collective-permute-done.26.refs_28_
  53.6 10.0 %shard_map.140 = (bf16[128,1152]{1,0:T(8,128)(2,1)S(1)}, bf16[1792,128]{1,0:T(8,128)(2,1)S(1)}, bf16[8,128,128]{2,1,0:T(8,128)(2,1)S(1)}, bf16[128,2304]{1,0:T(8...) custom-call(s32[4,8]{1,0:T(4,128)S(1)} %get-tuple-element.19.clips, ...), custom_call_target="tpu_custom_call" | custom-call | tf_op jit(solution)/shard_map/pallas_call | solution.py:333
  63.6 13.4 %all_to_all.15 = bf16[8,16,2304]{2,1,0:T(8,128)(2,1)S(1)} all-to-all(bf16[8,16,2304]{2,1,0:T(8,128)(2,1)S(1)} %bitcast.9), channel_id=1, replica_groups={{0,1,2,3,4,5,6,7},{8,9,10,11,12,13,14,15},{16,17,18,19,20,21,22,23},{24..., dimensions={0} | all-to-all | bytes 1179648 | tf_op jit(solution)/shard_map/all_to_all | solution.py:496
  76.9 3.1 %shard_map.141 = bf16[128,2304]{1,0:T(8,128)(2,1)S(1)} custom-call(s32[4,8]{1,0:T(4,128)S(1)} %get-tuple-element.19.clips, bf16[128,2304]{1,0:T(8,128)(2,1)S(1)} %bitcast.7), custom_call_target="tpu_custom_call" | custom-call | tf_op jit(solution)/shard_map/pallas_call | solution.py:333
  80.1 12.8 %all_to_all.16 = bf16[8,16,2304]{2,1,0:T(8,128)(2,1)S(1)} all-to-all(bf16[8,16,2304]{2,1,0:T(8,128)(2,1)S(1)} %bitcast.8), channel_id=1, replica_groups={{0,1,2,3,4,5,6,7},{8,9,10,11,12,13,14,15},{16,17,18,19,20,21,22,23},{24..., dimensions={0} | all-to-all | bytes 1179648 | tf_op jit(solution)/shard_map/all_to_all | solution.py:496
  92.8 6.8 %shard_map.142 = (bf16[128,1152]{1,0:T(8,128)(2,1)}, bf16[128,1152]{1,0:T(8,128)(2,1)}, bf16[32,2,1152]{2,1,0:T(2,128)(2,1)S(1)}) custom-call(s32[4,8]{1,0:T(4,128)S(1)} %get-tuple-element.19.clips, bf16[128,2304]{1,0:T(8,128)(2,1)S(1)} %bitcast.6, bf16[2,128,1152]{2,1,0:T(8,128)(2,1)S(1)} %get-tuple-element.20.tokens, ...), custom_call_target="tpu_custom_call" | custom-call | tf_op jit(solution)/shard_map/pallas_call | solution.py:333
  99.6 11.6 %all_to_all.17 = bf16[32,2,1152]{2,1,0:T(2,128)(2,1)S(1)} all-to-all(bf16[32,2,1152]{2,1,0:T(2,128)(2,1)S(1)} %get-tuple-element.34), channel_id=1, replica_groups=mesh['dp'=2,'ctx'=16] {'dp','ctx'}, dimensions={0} | all-to-all | bytes 294912 | tf_op jit(solution)/shard_map/all_to_all | solution.py:540
  (43 shorter events, 4.3 us)
Async XLA Ops:
  2.0 8.1 %collective-permute-start.5 = (bf16[144,1152]{1,0:T(8,128)(2,1)S(1)}, bf16[144,1152]{1,0:T(8,128)(2,1)S(1)}, u32[]{:S(2)}, u32[]{:S(2)}) collective-permute-start(bf16[144,1152]{1,0:T(8,128)(2,1)S(1)} %get-tuple-element.36.refs_0_), channel_id=1, source_target_pairs={{0,4},{1,3},{4,8},{5,1},{8,12},{9,5},{12,14},{13,9},{14,10},{15,13... | collective-permute-start | bytes 995336 | tf_op jit(solution)/shard_map/ppermute | solution.py:360
  5.0 8.8 %collective-permute-start = (bf16[144,1152]{1,0:T(8,128)(2,1)S(1)}, bf16[144,1152]{1,0:T(8,128)(2,1)S(1)}, u32[]{:S(2)}, u32[]{:S(2)}) collective-permute-start(bf16[144,1152]{1,0:T(8,128)(2,1)S(1)} %get-tuple-element.36.refs_0_), channel_id=1, source_target_pairs={{0,1},{1,0},{2,3},{3,2},{4,5},{5,4},{6,7},{7,6},{8,9},{9,8},{10,11... | collective-permute-start | bytes 995336 | tf_op jit(solution)/shard_map/ppermute | solution.py:366
  10.1 9.0 %collective-permute-start.16 = (bf16[144,1152]{1,0:T(8,128)(2,1)S(1)}, bf16[144,1152]{1,0:T(8,128)(2,1)S(1)}, u32[]{:S(2)}, u32[]{:S(2)}) collective-permute-start(bf16[144,1152]{1,0:T(8,128)(2,1)S(1)} %collective-permute-done.5.refs_2_), channel_id=1, source_target_pairs={{0,16},{16,0},{1,17},{17,1},{2,18},{18,2},{3,19},{19,3},{4,20},{20... | collective-permute-start | bytes 995336 | tf_op jit(solution)/shard_map/ppermute | solution.py:363
  12.1 7.0 %collective-permute-start.4 = (bf16[144,1152]{1,0:T(8,128)(2,1)S(1)}, bf16[144,1152]{1,0:T(8,128)(2,1)S(1)}, u32[]{:S(2)}, u32[]{:S(2)}) collective-permute-start(bf16[144,1152]{1,0:T(8,128)(2,1)S(1)} %get-tuple-element.35.refs_16_), channel_id=1, source_target_pairs={{0,1},{1,0},{2,3},{3,2},{4,5},{5,4},{6,7},{7,6},{8,9},{9,8},{10,11... | collective-permute-start | bytes 995336 | tf_op jit(solution)/shard_map/ppermute | solution.py:366
  12.1 8.8 %collective-permute-start.7 = (bf16[144,1152]{1,0:T(8,128)(2,1)S(1)}, bf16[144,1152]{1,0:T(8,128)(2,1)S(1)}, u32[]{:S(2)}, u32[]{:S(2)}) collective-permute-start(bf16[144,1152]{1,0:T(8,128)(2,1)S(1)} %collective-permute-done.5.refs_2_), channel_id=1, source_target_pairs={{0,4},{1,3},{4,8},{5,1},{8,12},{9,5},{12,14},{13,9},{14,10},{15,13... | collective-permute-start | bytes 995336 | tf_op jit(solution)/shard_map/ppermute | solution.py:360
  13.6 7.4 %collective-permute-start.6 = (bf16[144,1152]{1,0:T(8,128)(2,1)S(1)}, bf16[144,1152]{1,0:T(8,128)(2,1)S(1)}, u32[]{:S(2)}, u32[]{:S(2)}) collective-permute-start(bf16[144,1152]{1,0:T(8,128)(2,1)S(1)} %collective-permute-done.5.refs_2_), channel_id=1, source_target_pairs={{0,1},{1,0},{2,3},{3,2},{4,5},{5,4},{6,7},{7,6},{8,9},{9,8},{10,11... | collective-permute-start | bytes 995336 | tf_op jit(solution)/shard_map/ppermute | solution.py:366
  13.8 8.9 %collective-permute-start.1 = (bf16[144,1152]{1,0:T(8,128)(2,1)S(1)}, bf16[144,1152]{1,0:T(8,128)(2,1)S(1)}, u32[]{:S(2)}, u32[]{:S(2)}) collective-permute-start(bf16[144,1152]{1,0:T(8,128)(2,1)S(1)} %collective-permute-done.refs_1_), channel_id=1, source_target_pairs={{0,4},{1,3},{4,8},{5,1},{8,12},{9,5},{12,14},{13,9},{14,10},{15,13... | collective-permute-start | bytes 995336 | tf_op jit(solution)/shard_map/ppermute | solution.py:360
  19.1 4.9 %collective-permute-start.23 = (bf16[144,1152]{1,0:T(8,128)(2,1)S(1)}, bf16[144,1152]{1,0:T(8,128)(2,1)S(1)}, u32[]{:S(2)}, u32[]{:S(2)}) collective-permute-start(bf16[144,1152]{1,0:T(8,128)(2,1)S(1)} %collective-permute-done.16.refs_18_), channel_id=1, source_target_pairs={{0,1},{1,0},{2,3},{3,2},{4,5},{5,4},{6,7},{7,6},{8,9},{9,8},{10,11... | collective-permute-start | bytes 995336 | tf_op jit(solution)/shard_map/ppermute | solution.py:366
  19.1 7.2 %collective-permute-start.17 = (bf16[144,1152]{1,0:T(8,128)(2,1)S(1)}, bf16[144,1152]{1,0:T(8,128)(2,1)S(1)}, u32[]{:S(2)}, u32[]{:S(2)}) collective-permute-start(bf16[144,1152]{1,0:T(8,128)(2,1)S(1)} %collective-permute-done.16.refs_18_), channel_id=1, source_target_pairs={{0,4},{1,3},{4,8},{5,1},{8,12},{9,5},{12,14},{13,9},{14,10},{15,13... | collective-permute-start | bytes 995336 | tf_op jit(solution)/shard_map/ppermute | solution.py:360
  20.8 7.1 %collective-permute-start.11 = (bf16[144,1152]{1,0:T(8,128)(2,1)S(1)}, bf16[144,1152]{1,0:T(8,128)(2,1)S(1)}, u32[]{:S(2)}, u32[]{:S(2)}) collective-permute-start(bf16[144,1152]{1,0:T(8,128)(2,1)S(1)} %collective-permute-done.7.refs_3_), channel_id=1, source_target_pairs={{0,1},{1,0},{2,3},{3,2},{4,5},{5,4},{6,7},{7,6},{8,9},{9,8},{10,11... | collective-permute-start | bytes 995336 | tf_op jit(solution)/shard_map/ppermute | solution.py:366
  21.0 8.8 %collective-permute-start.8 = (bf16[144,1152]{1,0:T(8,128)(2,1)S(1)}, bf16[144,1152]{1,0:T(8,128)(2,1)S(1)}, u32[]{:S(2)}, u32[]{:S(2)}) collective-permute-start(bf16[144,1152]{1,0:T(8,128)(2,1)S(1)} %collective-permute-done.7.refs_3_), channel_id=1, source_target_pairs={{0,4},{1,3},{4,8},{5,1},{8,12},{9,5},{12,14},{13,9},{14,10},{15,13... | collective-permute-start | bytes 995336 | tf_op jit(solution)/shard_map/ppermute | solution.py:360
  22.7 9.4 %collective-permute-start.20 = (bf16[144,1152]{1,0:T(8,128)(2,1)S(1)}, bf16[144,1152]{1,0:T(8,128)(2,1)S(1)}, u32[]{:S(2)}, u32[]{:S(2)}) collective-permute-start(bf16[144,1152]{1,0:T(8,128)(2,1)S(1)} %collective-permute-done.1.refs_6_), channel_id=1, source_target_pairs={{0,16},{16,0},{1,17},{17,1},{2,18},{18,2},{3,19},{19,3},{4,20},{20... | collective-permute-start | bytes 995336 | tf_op jit(solution)/shard_map/ppermute | solution.py:363
  24.0 8.1 %collective-permute-start.3 = (bf16[144,1152]{1,0:T(8,128)(2,1)S(1)}, bf16[144,1152]{1,0:T(8,128)(2,1)S(1)}, u32[]{:S(2)}, u32[]{:S(2)}) collective-permute-start(bf16[144,1152]{1,0:T(8,128)(2,1)S(1)} %collective-permute-done.1.refs_6_), channel_id=1, source_target_pairs={{0,1},{1,0},{2,3},{3,2},{4,5},{5,4},{6,7},{7,6},{8,9},{9,8},{10,11... | collective-permute-start | bytes 995336 | tf_op jit(solution)/shard_map/ppermute | solution.py:366
  26.3 7.4 %collective-permute-start.2 = (bf16[144,1152]{1,0:T(8,128)(2,1)S(1)}, bf16[144,1152]{1,0:T(8,128)(2,1)S(1)}, u32[]{:S(2)}, u32[]{:S(2)}) collective-permute-start(bf16[144,1152]{1,0:T(8,128)(2,1)S(1)} %collective-permute-done.1.refs_6_), channel_id=1, source_target_pairs={{0,4},{1,3},{4,8},{5,1},{8,12},{9,5},{12,14},{13,9},{14,10},{15,13... | collective-permute-start | bytes 995336 | tf_op jit(solution)/shard_map/ppermute | solution.py:360
  28.0 5.9 %collective-permute-start.24 = (bf16[144,1152]{1,0:T(8,128)(2,1)S(1)}, bf16[144,1152]{1,0:T(8,128)(2,1)S(1)}, u32[]{:S(2)}, u32[]{:S(2)}) collective-permute-start(bf16[144,1152]{1,0:T(8,128)(2,1)S(1)} %collective-permute-done.17.refs_19_), channel_id=1, source_target_pairs={{0,1},{1,0},{2,3},{3,2},{4,5},{5,4},{6,7},{7,6},{8,9},{9,8},{10,11... | collective-permute-start | bytes 995336 | tf_op jit(solution)/shard_map/ppermute | solution.py:366
  29.8 9.8 %collective-permute-start.18 = (bf16[144,1152]{1,0:T(8,128)(2,1)S(1)}, bf16[144,1152]{1,0:T(8,128)(2,1)S(1)}, u32[]{:S(2)}, u32[]{:S(2)}) collective-permute-start(bf16[144,1152]{1,0:T(8,128)(2,1)S(1)} %collective-permute-done.8.refs_4_), channel_id=1, source_target_pairs={{0,16},{16,0},{1,17},{17,1},{2,18},{18,2},{3,19},{19,3},{4,20},{20... | collective-permute-start | bytes 995336 | tf_op jit(solution)/shard_map/ppermute | solution.py:363
  32.1 7.6 %collective-permute-start.12 = (bf16[144,1152]{1,0:T(8,128)(2,1)S(1)}, bf16[144,1152]{1,0:T(8,128)(2,1)S(1)}, u32[]{:S(2)}, u32[]{:S(2)}) collective-permute-start(bf16[144,1152]{1,0:T(8,128)(2,1)S(1)} %collective-permute-done.8.refs_4_), channel_id=1, source_target_pairs={{0,1},{1,0},{2,3},{3,2},{4,5},{5,4},{6,7},{7,6},{8,9},{9,8},{10,11... | collective-permute-start | bytes 995336 | tf_op jit(solution)/shard_map/ppermute | solution.py:366
  32.1 9.2 %collective-permute-start.9 = (bf16[144,1152]{1,0:T(8,128)(2,1)S(1)}, bf16[144,1152]{1,0:T(8,128)(2,1)S(1)}, u32[]{:S(2)}, u32[]{:S(2)}) collective-permute-start(bf16[144,1152]{1,0:T(8,128)(2,1)S(1)} %collective-permute-done.8.refs_4_), channel_id=1, source_target_pairs={{0,4},{1,3},{4,8},{5,1},{8,12},{9,5},{12,14},{13,9},{14,10},{15,13... | collective-permute-start | bytes 995336 | tf_op jit(solution)/shard_map/ppermute | solution.py:360
  33.7 7.6 %collective-permute-start.27 = (bf16[144,1152]{1,0:T(8,128)(2,1)S(1)}, bf16[144,1152]{1,0:T(8,128)(2,1)S(1)}, u32[]{:S(2)}, u32[]{:S(2)}) collective-permute-start(bf16[144,1152]{1,0:T(8,128)(2,1)S(1)} %collective-permute-done.20.refs_22_), channel_id=1, source_target_pairs={{0,1},{1,0},{2,3},{3,2},{4,5},{5,4},{6,7},{7,6},{8,9},{9,8},{10,11... | collective-permute-start | bytes 995336 | tf_op jit(solution)/shard_map/ppermute | solution.py:366
  33.9 8.9 %collective-permute-start.21 = (bf16[144,1152]{1,0:T(8,128)(2,1)S(1)}, bf16[144,1152]{1,0:T(8,128)(2,1)S(1)}, u32[]{:S(2)}, u32[]{:S(2)}) collective-permute-start(bf16[144,1152]{1,0:T(8,128)(2,1)S(1)} %collective-permute-done.20.refs_22_), channel_id=1, source_target_pairs={{0,4},{1,3},{4,8},{5,1},{8,12},{9,5},{12,14},{13,9},{14,10},{15,13... | collective-permute-start | bytes 995336 | tf_op jit(solution)/shard_map/ppermute | solution.py:360
  39.7 4.7 %collective-permute-start.14 = (bf16[144,1152]{1,0:T(8,128)(2,1)S(1)}, bf16[144,1152]{1,0:T(8,128)(2,1)S(1)}, u32[]{:S(2)}, u32[]{:S(2)}) collective-permute-start(bf16[144,1152]{1,0:T(8,128)(2,1)S(1)} %get-tuple-element.22.refs_7_), channel_id=1, source_target_pairs={{0,1},{1,0},{2,3},{3,2},{4,5},{5,4},{6,7},{7,6},{8,9},{9,8},{10,11... | collective-permute-start | bytes 995336 | tf_op jit(solution)/shard_map/ppermute | solution.py:366
  39.7 7.1 %collective-permute-start.10 = (bf16[144,1152]{1,0:T(8,128)(2,1)S(1)}, bf16[144,1152]{1,0:T(8,128)(2,1)S(1)}, u32[]{:S(2)}, u32[]{:S(2)}) collective-permute-start(bf16[144,1152]{1,0:T(8,128)(2,1)S(1)} %get-tuple-element.22.refs_7_), channel_id=1, source_target_pairs={{0,4},{1,3},{4,8},{5,1},{8,12},{9,5},{12,14},{13,9},{14,10},{15,13... | collective-permute-start | bytes 995336 | tf_op jit(solution)/shard_map/ppermute | solution.py:360
  41.3 5.5 %collective-permute-start.25 = (bf16[144,1152]{1,0:T(8,128)(2,1)S(1)}, bf16[144,1152]{1,0:T(8,128)(2,1)S(1)}, u32[]{:S(2)}, u32[]{:S(2)}) collective-permute-start(bf16[144,1152]{1,0:T(8,128)(2,1)S(1)} %collective-permute-done.18.refs_20_), channel_id=1, source_target_pairs={{0,1},{1,0},{2,3},{3,2},{4,5},{5,4},{6,7},{7,6},{8,9},{9,8},{10,11... | collective-permute-start | bytes 995336 | tf_op jit(solution)/shard_map/ppermute | solution.py:366
  41.3 10.2 %collective-permute-start.19 = (bf16[144,1152]{1,0:T(8,128)(2,1)S(1)}, bf16[144,1152]{1,0:T(8,128)(2,1)S(1)}, u32[]{:S(2)}, u32[]{:S(2)}) collective-permute-start(bf16[144,1152]{1,0:T(8,128)(2,1)S(1)} %collective-permute-done.9.refs_5_), channel_id=1, source_target_pairs={{0,16},{16,0},{1,17},{17,1},{2,18},{18,2},{3,19},{19,3},{4,20},{20... | collective-permute-start | bytes 995336 | tf_op jit(solution)/shard_map/ppermute | solution.py:363
  42.8 8.7 %collective-permute-start.22 = (bf16[144,1152]{1,0:T(8,128)(2,1)S(1)}, bf16[144,1152]{1,0:T(8,128)(2,1)S(1)}, u32[]{:S(2)}, u32[]{:S(2)}) collective-permute-start(bf16[144,1152]{1,0:T(8,128)(2,1)S(1)} %collective-permute-done.21.refs_23_), channel_id=1, source_target_pairs={{0,4},{1,3},{4,8},{5,1},{8,12},{9,5},{12,14},{13,9},{14,10},{15,13... | collective-permute-start | bytes 995336 | tf_op jit(solution)/shard_map/ppermute | solution.py:360
  44.4 7.6 %collective-permute-start.13 = (bf16[144,1152]{1,0:T(8,128)(2,1)S(1)}, bf16[144,1152]{1,0:T(8,128)(2,1)S(1)}, u32[]{:S(2)}, u32[]{:S(2)}) collective-permute-start(bf16[144,1152]{1,0:T(8,128)(2,1)S(1)} %collective-permute-done.9.refs_5_), channel_id=1, source_target_pairs={{0,1},{1,0},{2,3},{3,2},{4,5},{5,4},{6,7},{7,6},{8,9},{9,8},{10,11... | collective-permute-start | bytes 995336 | tf_op jit(solution)/shard_map/ppermute | solution.py:366
  46.8 5.2 %collective-permute-start.28 = (bf16[144,1152]{1,0:T(8,128)(2,1)S(1)}, bf16[144,1152]{1,0:T(8,128)(2,1)S(1)}, u32[]{:S(2)}, u32[]{:S(2)}) collective-permute-start(bf16[144,1152]{1,0:T(8,128)(2,1)S(1)} %collective-permute-done.21.refs_23_), channel_id=1, source_target_pairs={{0,1},{1,0},{2,3},{3,2},{4,5},{5,4},{6,7},{7,6},{8,9},{9,8},{10,11... | collective-permute-start | bytes 995336 | tf_op jit(solution)/shard_map/ppermute | solution.py:366
  46.8 5.2 %collective-permute-start.15 = (bf16[144,1152]{1,0:T(8,128)(2,1)S(1)}, bf16[144,1152]{1,0:T(8,128)(2,1)S(1)}, u32[]{:S(2)}, u32[]{:S(2)}) collective-permute-start(bf16[144,1152]{1,0:T(8,128)(2,1)S(1)} %collective-permute-done.10.refs_8_), channel_id=1, source_target_pairs={{0,1},{1,0},{2,3},{3,2},{4,5},{5,4},{6,7},{7,6},{8,9},{9,8},{10,11... | collective-permute-start | bytes 995336 | tf_op jit(solution)/shard_map/ppermute | solution.py:366
  51.5 1.6 %collective-permute-start.26 = (bf16[144,1152]{1,0:T(8,128)(2,1)S(1)}, bf16[144,1152]{1,0:T(8,128)(2,1)S(1)}, u32[]{:S(2)}, u32[]{:S(2)}) collective-permute-start(bf16[144,1152]{1,0:T(8,128)(2,1)S(1)} %collective-permute-done.19.refs_21_), channel_id=1, source_target_pairs={{0,1},{1,0},{2,3},{3,2},{4,5},{5,4},{6,7},{7,6},{8,9},{9,8},{10,11... | collective-permute-start | bytes 995336 | tf_op jit(solution)/shard_map/ppermute | solution.py:366
  51.5 2.1 %collective-permute-start.29 = (bf16[144,1152]{1,0:T(8,128)(2,1)S(1)}, bf16[144,1152]{1,0:T(8,128)(2,1)S(1)}, u32[]{:S(2)}, u32[]{:S(2)}) collective-permute-start(bf16[144,1152]{1,0:T(8,128)(2,1)S(1)} %collective-permute-done.22.refs_24_), channel_id=1, source_target_pairs={{0,1},{1,0},{2,3},{3,2},{4,5},{5,4},{6,7},{7,6},{8,9},{9,8},{10,11... | collective-permute-start | bytes 995336 | tf_op jit(solution)/shard_map/ppermute | solution.py:366

commit v2 on v1

--- a/solution.py
+++ b/solution.py
@@ -12,6 +12,7 @@
 FRAME = 128
 EPSILON = 1e-06
 ROPE_BASE = 10000.0
+MASKED = -1e30
 F32 = jnp.float32
 BF16 = jnp.bfloat16
 VMEM_LIMIT = 12 * 1024 * 1024
@@ -99,17 +100,24 @@
 
 
 def shares_of(queries, keys, allowed, live, scale):
-    scores = tn(keys, queries) * scale
-    weights = jnp.where(allowed, jnp.exp(jnp.where(allowed, scores, 0.0)), 0.0)
-    totals = jnp.sum(weights, axis=0, keepdims=True) + (1.0 - live)
-    return weights * (1.0 / totals)
-
-
-def attend_back(queries, keys, values, shares, shares_low, grad, scale):
-    grad_shares = tn(values, grad)
-    middle = jnp.sum(shares * grad_shares, axis=0, keepdims=True)
-    grad_scores = (shares * (grad_shares - middle) * scale).astype(BF16)
-    return nn(keys, grad_scores), nt(queries, grad_scores), nt(grad, shares_low)
+    scores = [tn(key, query) for key, query in zip(keys, queries)]
+    weights = [jnp.exp(jnp.where(allowed, score * scale, MASKED)) for score in scores]
+    totals = [jnp.sum(weight, axis=0, keepdims=True) + (1.0 - live) for weight in weights]
+    return [weight * (1.0 / total) for weight, total in zip(weights, totals)]
+
+
+def attend_back(queries, keys, values, shares, shares_low, grads, scale):
+    grad_shares = [tn(value, grad) for value, grad in zip(values, grads)]
+    middles = [jnp.sum(a * b, axis=0, keepdims=True) for a, b in zip(shares, grad_shares)]
+    grad_scores = [
+        (share * (grad_share - middle) * scale).astype(BF16)
+        for share, grad_share, middle in zip(shares, grad_shares, middles)
+    ]
+    return (
+        [nn(key, grad_score) for key, grad_score in zip(keys, grad_scores)],
+        [nt(query, grad_score) for query, grad_score in zip(queries, grad_scores)],
+        [nt(grad, share) for grad, share in zip(grads, shares_low)],
+    )
 
 
 def clips_at(clips, frames):
@@ -145,12 +153,10 @@
 
 
 def turn_tables(times, half):
-    pair = ids((2 * half, FRAME), 0)
-    lower = pair < half
-    frequency = jnp.exp(jnp.where(lower, pair, pair - half).astype(F32) * (-math.log(ROPE_BASE) / half))
+    frequency = jnp.exp(ids((half, FRAME), 0).astype(F32) * (-math.log(ROPE_BASE) / half))
     angles = frequency * times
-    sine = jnp.sin(angles)
-    return jnp.cos(angles), jnp.where(lower, -sine, sine)
+    cosine, sine = jnp.cos(angles), jnp.sin(angles)
+    return jnp.concatenate([cosine, cosine], axis=0), jnp.concatenate([-sine, sine], axis=0)
 
 
 def out_columns(rows):
@@ -224,13 +230,15 @@
     pl.when(order[-1] != 0)(lambda: project_from(layouts[1]))
     saved[...] = project[...].astype(BF16)
     scale = rows.head ** (-0.5)
+    queries, keys, values_in = (
+        [read_rows(project, rows.qkv_spans(which, head, stride)).astype(BF16) for head in range(HEADS)]
+        for which in range(3)
+    )
+    shares = [share.astype(BF16) for share in shares_of(queries, keys, allowed, live, scale)]
+    blended = [nn(value, share) * live for value, share in zip(values_in, shares)]
     for head in range(HEADS):
-        query, key, value = (
-            read_rows(project, rows.qkv_spans(which, head, stride)).astype(BF16) for which in range(3)
-        )
-        shares = shares_of(query, key, allowed, live, scale).astype(BF16)
-        shares_out[head] = shares
-        write_rows(mixed, rows.out_spans(head, rows.out_cut), nn(value, shares) * live)
+        shares_out[head] = shares[head]
+        write_rows(mixed, rows.out_spans(head, rows.out_cut), blended[head])
     wait_weights(layouts, order, pieces, space, sems, 0)
     update = tn(mixed[...].astype(BF16), rows.out_weight(space))
     low = (values + update).astype(BF16)
@@ -254,26 +262,28 @@
     def swapped(vectors):
         return jnp.concatenate([vectors[half:], vectors[:half]], axis=0)
 
-    for head in range(HEADS):
-        turned = []
+    heads = range(HEADS)
+    turned = []
+    for which in range(2):
+        vectors = [read_rows(project, rows.qkv_spans(which, head, rows.shard)) for head in heads]
+        turned.append([(part * cosine + swapped(part) * sine).astype(BF16) for part in vectors])
+    queries, keys = turned
+    values = [read_rows(project, rows.qkv_spans(2, head, rows.shard)).astype(BF16) for head in heads]
+    grads = [(read_rows(project, rows.out_spans(head, 0)) * live).astype(BF16) for head in heads]
+    shares = shares_of(queries, keys, allowed, live, scale)
+    shares_low = [share.astype(BF16) for share in shares]
+    blended = [nn(value, share) * live for value, share in zip(values, shares_low)]
+    parts = attend_back(queries, keys, values, shares, shares_low, grads, scale)
+    for head in heads:
+        write_rows(result, rows.out_spans(head, 0), blended[head])
         for which in range(2):
-            vectors = read_rows(project, rows.qkv_spans(which, head, rows.shard))
-            turned.append((vectors * cosine + swapped(vectors) * sine).astype(BF16))
-        query, key = turned
-        value = read_rows(project, rows.qkv_spans(2, head, rows.shard)).astype(BF16)
-        grad = (read_rows(project, rows.out_spans(head, 0)) * live).astype(BF16)
-        shares = shares_of(query, key, allowed, live, scale)
-        shares_low = shares.astype(BF16)
-        write_rows(result, rows.out_spans(head, 0), nn(value, shares_low) * live)
-        grads = attend_back(query, key, value, shares, shares_low, grad, scale)
-        for which in range(2):
-            turned_grad = grads[which].astype(BF16).astype(F32)
+            turned_grad = parts[which][head].astype(BF16).astype(F32)
             write_rows(
                 result,
                 rows.qkv_spans(which, head, rows.shard),
                 turned_grad * cosine - swapped(turned_grad) * sine,
             )
-        write_rows(result, rows.qkv_spans(2, head, rows.shard), grads[2])
+        write_rows(result, rows.qkv_spans(2, head, rows.shard), parts[2][head])
     for first in range(0, rows.total, FRAME):
         sent[:, first : first + FRAME] = result[first : first + FRAME, :].T.astype(BF16)
 
@@ -311,13 +321,19 @@
     project[...] = nt(rows.out_weight(space), grad_hidden)
     grad_project[...] = jnp.zeros_like(grad_project)
     scale = rows.head ** (-0.5)
-    for head in range(HEADS):
-        spans = [rows.qkv_spans(which, head, rows.qkv_cut) for which in range(3)]
-        query, key, value = (read_rows(saved, where).astype(BF16) for where in spans)
-        grad = (read_rows(project, rows.out_spans(head, rows.out_cut)) * live).astype(BF16)
-        shares_low = shares_in[head]
-        grads = attend_back(query, key, value, shares_low.astype(F32), shares_low, grad, scale)
-        for where, part in zip(spans, grads):
+    heads = range(HEADS)
+    spans = [[rows.qkv_spans(which, head, rows.qkv_cut) for head in heads] for which in range(3)]
+    queries, keys, values_in = (
+        [read_rows(saved, where).astype(BF16) for where in places] for places in spans
+    )
+    grads = [
+        (read_rows(project, rows.out_spans(head, rows.out_cut)) * live).astype(BF16) for head in heads
+    ]
+    shares_low = [shares_in[head] for head in heads]
+    shares = [share.astype(F32) for share in shares_low]
+    parts = attend_back(queries, keys, values_in, shares, shares_low, grads, scale)
+    for places, found in zip(spans, parts):
+        for where, part in zip(places, found):
             write_rows(grad_project, where, part)
     grad_normed = tn(grad_project[...].astype(BF16), rows.qkv_weight(space)).astype(BF16).astype(F32)
     values = tokens[0].astype(F32)

time: 112 us -> 110 us (0.982)
  Pallas kernels: 19.9 us -> 17.4 us
    pallas_call x3, Pallas kernels: 19.9 us -> 17.4 us  [call(): pl.pallas_call(body, out_shape=out_shapes, in_specs=[scalars] + [whole] *...]
where the time goes in v2:
time: 110 us; the launch traced here: 109 us
  blocking collectives  37.8 us (34%)
  starting transfers between devices  25 us (23%)
  waiting for transfers between devices  23.3 us (21%)
  Pallas kernels  17.4 us (16%)
  other arithmetic  3.89 us (4%)
  local copies, waits for them, and re-layouts  1.4 us (1%)
    all_to_all x2, blocking collectives, exchange(): lax.all_to_all(sent.reshape(near, slots, rows.total), 'ctx', split_axis=0...  26.1 us
    pallas_call x3, Pallas kernels, call(): pl.pallas_call(body, out_shape=out_shapes, in_specs=[scalars] + [whole] *...  17.4 us
    ppermute x10, starting transfers between devices, ring(): return lax.ppermute(rows, 'ctx', ring_pairs)  17.1 us
    all_to_all x1, blocking collectives, shards(): lax.all_to_all(gains, ('dp', 'ctx'), split_axis=0, concat_axis=0, tiled=T...  11.7 us
    ppermute x4, waiting for transfers between devices, across(): lax.ppermute(rows, 'dp', [(index, index ^ 1) for index in range(planes)])  11.2 us
    ppermute x10, waiting for transfers between devices, ring(): return lax.ppermute(rows, 'ctx', ring_pairs)  10.5 us
    ppermute x4, starting transfers between devices, across(): lax.ppermute(rows, 'dp', [(index, index ^ 1) for index in range(planes)])  6.36 us
  transfers between devices with their start and end apart: 30, of which 11 were waited for; matrix products, arithmetic and copies ran while one was open for 3% of the time, Pallas kernels for 0%

profile of v2, /device:TPU:0, one launch (start us, length us, event | category | flops | bytes accessed | tf_op | source)
XLA Modules:
  0.0 109.5 jit_solution(17938997559762303436)
XLA Ops:
  0.6 1.3 %broadcast_select_fusion = (bf16[144,1152]{1,0:T(8,128)(2,1)S(1)}, bf16[144,1152]{1,0:T(8,128)(2,1)S(1)}) fusion(pred[]{:T(512)S(6)} %eq.4, bf16[36,1152]{1,0:T(8,128)(2,1)} %param.23, bf16[108,1152]{1,0:T(8,128)(2,1)} %param.22, bf16[36,1152]{1,0:T(8,128)(2,1)} %param.20, bf16[108,1152]{1,0:T(8,128)(2,1)} %param.19), kind=kLoop, calls=%fused_computation.3 | loop fusion | flops 1658880 | bytes 1327105 | tf_op jit(solution)/shard_map/jit(_where)/select_n | solution.py:385
  2.0 3.1 %collective-permute-start.5 = (bf16[144,1152]{1,0:T(8,128)(2,1)S(1)}, bf16[144,1152]{1,0:T(8,128)(2,1)S(1)}, u32[]{:S(2)}, u32[]{:S(2)}) collective-permute-start(bf16[144,1152]{1,0:T(8,128)(2,1)S(1)} %get-tuple-element.36.refs_0_), channel_id=1, source_target_pairs={{0,4},{1,3},{4,8},{5,1},{8,12},{9,5},{12,14},{13,9},{14,10},{15,13... | collective-permute-start | bytes 995336 | tf_op jit(solution)/shard_map/ppermute | solution.py:376
  5.0 5.0 %collective-permute-done.5.refs_2_ = bf16[144,1152]{1,0:T(8,128)(2,1)S(1)} collective-permute-done((bf16[144,1152]{1,0:T(8,128)(2,1)S(1)}, bf16[144,1152]{1,0:T(8,128)(2,1)S(1)}, u32[]{:S(2)}, u32[]{:S(2)}) %collective-permute-start.5) | collective-permute-done | bytes 331808 | tf_op jit(solution)/shard_map/ppermute | solution.py:376
  10.1 2.0 %collective-permute-start.16 = (bf16[144,1152]{1,0:T(8,128)(2,1)S(1)}, bf16[144,1152]{1,0:T(8,128)(2,1)S(1)}, u32[]{:S(2)}, u32[]{:S(2)}) collective-permute-start(bf16[144,1152]{1,0:T(8,128)(2,1)S(1)} %collective-permute-done.5.refs_2_), channel_id=1, source_target_pairs={{0,16},{16,0},{1,17},{17,1},{2,18},{18,2},{3,19},{19,3},{4,20},{20... | collective-permute-start | bytes 995336 | tf_op jit(solution)/shard_map/ppermute | solution.py:379
  12.1 1.6 %collective-permute-start.7 = (bf16[144,1152]{1,0:T(8,128)(2,1)S(1)}, bf16[144,1152]{1,0:T(8,128)(2,1)S(1)}, u32[]{:S(2)}, u32[]{:S(2)}) collective-permute-start(bf16[144,1152]{1,0:T(8,128)(2,1)S(1)} %collective-permute-done.5.refs_2_), channel_id=1, source_target_pairs={{0,4},{1,3},{4,8},{5,1},{8,12},{9,5},{12,14},{13,9},{14,10},{15,13... | collective-permute-start | bytes 995336 | tf_op jit(solution)/shard_map/ppermute | solution.py:376
  13.8 1.4 %collective-permute-start.1 = (bf16[144,1152]{1,0:T(8,128)(2,1)S(1)}, bf16[144,1152]{1,0:T(8,128)(2,1)S(1)}, u32[]{:S(2)}, u32[]{:S(2)}) collective-permute-start(bf16[144,1152]{1,0:T(8,128)(2,1)S(1)} %collective-permute-done.refs_1_), channel_id=1, source_target_pairs={{0,4},{1,3},{4,8},{5,1},{8,12},{9,5},{12,14},{13,9},{14,10},{15,13... | collective-permute-start | bytes 995336 | tf_op jit(solution)/shard_map/ppermute | solution.py:376
  15.2 3.9 %collective-permute-done.16.refs_18_ = bf16[144,1152]{1,0:T(8,128)(2,1)S(1)} collective-permute-done((bf16[144,1152]{1,0:T(8,128)(2,1)S(1)}, bf16[144,1152]{1,0:T(8,128)(2,1)S(1)}, u32[]{:S(2)}, u32[]{:S(2)}) %collective-permute-start.16) | collective-permute-done | bytes 331808 | tf_op jit(solution)/shard_map/ppermute | solution.py:379
  19.1 1.7 %collective-permute-start.17 = (bf16[144,1152]{1,0:T(8,128)(2,1)S(1)}, bf16[144,1152]{1,0:T(8,128)(2,1)S(1)}, u32[]{:S(2)}, u32[]{:S(2)}) collective-permute-start(bf16[144,1152]{1,0:T(8,128)(2,1)S(1)} %collective-permute-done.16.refs_18_), channel_id=1, source_target_pairs={{0,4},{1,3},{4,8},{5,1},{8,12},{9,5},{12,14},{13,9},{14,10},{15,13... | collective-permute-start | bytes 995336 | tf_op jit(solution)/shard_map/ppermute | solution.py:376
  21.0 1.5 %collective-permute-start.8 = (bf16[144,1152]{1,0:T(8,128)(2,1)S(1)}, bf16[144,1152]{1,0:T(8,128)(2,1)S(1)}, u32[]{:S(2)}, u32[]{:S(2)}) collective-permute-start(bf16[144,1152]{1,0:T(8,128)(2,1)S(1)} %collective-permute-done.7.refs_3_), channel_id=1, source_target_pairs={{0,4},{1,3},{4,8},{5,1},{8,12},{9,5},{12,14},{13,9},{14,10},{15,13... | collective-permute-start | bytes 995336 | tf_op jit(solution)/shard_map/ppermute | solution.py:376
  22.7 1.2 %collective-permute-start.20 = (bf16[144,1152]{1,0:T(8,128)(2,1)S(1)}, bf16[144,1152]{1,0:T(8,128)(2,1)S(1)}, u32[]{:S(2)}, u32[]{:S(2)}) collective-permute-start(bf16[144,1152]{1,0:T(8,128)(2,1)S(1)} %collective-permute-done.1.refs_6_), channel_id=1, source_target_pairs={{0,16},{16,0},{1,17},{17,1},{2,18},{18,2},{3,19},{19,3},{4,20},{20... | collective-permute-start | bytes 995336 | tf_op jit(solution)/shard_map/ppermute | solution.py:379
  24.0 2.3 %collective-permute-done.17.refs_19_ = bf16[144,1152]{1,0:T(8,128)(2,1)S(1)} collective-permute-done((bf16[144,1152]{1,0:T(8,128)(2,1)S(1)}, bf16[144,1152]{1,0:T(8,128)(2,1)S(1)}, u32[]{:S(2)}, u32[]{:S(2)}) %collective-permute-start.17) | collective-permute-done | bytes 331808 | tf_op jit(solution)/shard_map/ppermute | solution.py:376
  26.3 1.7 %collective-permute-start.2 = (bf16[144,1152]{1,0:T(8,128)(2,1)S(1)}, bf16[144,1152]{1,0:T(8,128)(2,1)S(1)}, u32[]{:S(2)}, u32[]{:S(2)}) collective-permute-start(bf16[144,1152]{1,0:T(8,128)(2,1)S(1)} %collective-permute-done.1.refs_6_), channel_id=1, source_target_pairs={{0,4},{1,3},{4,8},{5,1},{8,12},{9,5},{12,14},{13,9},{14,10},{15,13... | collective-permute-start | bytes 995336 | tf_op jit(solution)/shard_map/ppermute | solution.py:376
  28.0 0.7 stack.9
  28.7 0.7 stack.10
  29.8 1.6 %collective-permute-start.18 = (bf16[144,1152]{1,0:T(8,128)(2,1)S(1)}, bf16[144,1152]{1,0:T(8,128)(2,1)S(1)}, u32[]{:S(2)}, u32[]{:S(2)}) collective-permute-start(bf16[144,1152]{1,0:T(8,128)(2,1)S(1)} %collective-permute-done.8.refs_4_), channel_id=1, source_target_pairs={{0,16},{16,0},{1,17},{17,1},{2,18},{18,2},{3,19},{19,3},{4,20},{20... | collective-permute-start | bytes 995336 | tf_op jit(solution)/shard_map/ppermute | solution.py:379
  32.1 1.6 %collective-permute-start.9 = (bf16[144,1152]{1,0:T(8,128)(2,1)S(1)}, bf16[144,1152]{1,0:T(8,128)(2,1)S(1)}, u32[]{:S(2)}, u32[]{:S(2)}) collective-permute-start(bf16[144,1152]{1,0:T(8,128)(2,1)S(1)} %collective-permute-done.8.refs_4_), channel_id=1, source_target_pairs={{0,4},{1,3},{4,8},{5,1},{8,12},{9,5},{12,14},{13,9},{14,10},{15,13... | collective-permute-start | bytes 995336 | tf_op jit(solution)/shard_map/ppermute | solution.py:376
  33.9 1.4 %collective-permute-start.21 = (bf16[144,1152]{1,0:T(8,128)(2,1)S(1)}, bf16[144,1152]{1,0:T(8,128)(2,1)S(1)}, u32[]{:S(2)}, u32[]{:S(2)}) collective-permute-start(bf16[144,1152]{1,0:T(8,128)(2,1)S(1)} %collective-permute-done.20.refs_22_), channel_id=1, source_target_pairs={{0,4},{1,3},{4,8},{5,1},{8,12},{9,5},{12,14},{13,9},{14,10},{15,13... | collective-permute-start | bytes 995336 | tf_op jit(solution)/shard_map/ppermute | solution.py:376
  35.3 0.7 pad_add_fusion.refs_6_
  36.0 1.1 %pad_maximum_fusion.refs_4_ = bf16[2,128,1152]{2,1,0:T(8,128)(2,1)S(1)} fusion(bf16[1,128,1152]{2,1,0:T(8,128)(2,1)} %param.13, bf16[1,128,1152]{2,1,0:T(8,128)(2,1)} %param.12), kind=kLoop, calls=%fused_computation | loop fusion | flops 294912 | bytes 1179648 | tf_op jit(solution)/shard_map/concatenate | solution.py:493
  37.2 2.5 %collective-permute-done.18.refs_20_ = bf16[144,1152]{1,0:T(8,128)(2,1)S(1)} collective-permute-done((bf16[144,1152]{1,0:T(8,128)(2,1)S(1)}, bf16[144,1152]{1,0:T(8,128)(2,1)S(1)}, u32[]{:S(2)}, u32[]{:S(2)}) %collective-permute-start.18) | collective-permute-done | bytes 331808 | tf_op jit(solution)/shard_map/ppermute | solution.py:379
  39.7 1.6 %collective-permute-start.10 = (bf16[144,1152]{1,0:T(8,128)(2,1)S(1)}, bf16[144,1152]{1,0:T(8,128)(2,1)S(1)}, u32[]{:S(2)}, u32[]{:S(2)}) collective-permute-start(bf16[144,1152]{1,0:T(8,128)(2,1)S(1)} %get-tuple-element.22.refs_7_), channel_id=1, source_target_pairs={{0,4},{1,3},{4,8},{5,1},{8,12},{9,5},{12,14},{13,9},{14,10},{15,13... | collective-permute-start | bytes 995336 | tf_op jit(solution)/shard_map/ppermute | solution.py:376
  41.3 1.6 %collective-permute-start.19 = (bf16[144,1152]{1,0:T(8,128)(2,1)S(1)}, bf16[144,1152]{1,0:T(8,128)(2,1)S(1)}, u32[]{:S(2)}, u32[]{:S(2)}) collective-permute-start(bf16[144,1152]{1,0:T(8,128)(2,1)S(1)} %collective-permute-done.9.refs_5_), channel_id=1, source_target_pairs={{0,16},{16,0},{1,17},{17,1},{2,18},{18,2},{3,19},{19,3},{4,20},{20... | collective-permute-start | bytes 995336 | tf_op jit(solution)/shard_map/ppermute | solution.py:379
  42.8 1.6 %collective-permute-start.22 = (bf16[144,1152]{1,0:T(8,128)(2,1)S(1)}, bf16[144,1152]{1,0:T(8,128)(2,1)S(1)}, u32[]{:S(2)}, u32[]{:S(2)}) collective-permute-start(bf16[144,1152]{1,0:T(8,128)(2,1)S(1)} %collective-permute-done.21.refs_23_), channel_id=1, source_target_pairs={{0,4},{1,3},{4,8},{5,1},{8,12},{9,5},{12,14},{13,9},{14,10},{15,13... | collective-permute-start | bytes 995336 | tf_op jit(solution)/shard_map/ppermute | solution.py:376
  44.4 2.4 %collective-permute-done.10.refs_8_ = bf16[144,1152]{1,0:T(8,128)(2,1)S(1)} collective-permute-done((bf16[144,1152]{1,0:T(8,128)(2,1)S(1)}, bf16[144,1152]{1,0:T(8,128)(2,1)S(1)}, u32[]{:S(2)}, u32[]{:S(2)}) %collective-permute-start.10) | collective-permute-done | bytes 331808 | tf_op jit(solution)/shard_map/ppermute | solution.py:376
  47.3 4.2 %collective-permute-done.19.refs_21_ = bf16[144,1152]{1,0:T(8,128)(2,1)S(1)} collective-permute-done((bf16[144,1152]{1,0:T(8,128)(2,1)S(1)}, bf16[144,1152]{1,0:T(8,128)(2,1)S(1)}, u32[]{:S(2)}, u32[]{:S(2)}) %collective-permute-start.19) | collective-permute-done | bytes 331808 | tf_op jit(solution)/shard_map/ppermute | solution.py:379
  52.0 1.1 %collective-permute-done.26.refs_28_ = bf16[144,1152]{1,0:T(8,128)(2,1)S(1)} collective-permute-done((bf16[144,1152]{1,0:T(8,128)(2,1)S(1)}, bf16[144,1152]{1,0:T(8,128)(2,1)S(1)}, u32[]{:S(2)}, u32[]{:S(2)}) %collective-permute-start.26) | collective-permute-done | bytes 331808 | tf_op jit(solution)/shard_map/ppermute | solution.py:382
  53.6 9.7 %shard_map.140 = (bf16[128,1152]{1,0:T(8,128)(2,1)S(1)}, bf16[1792,128]{1,0:T(8,128)(2,1)S(1)}, bf16[8,128,128]{2,1,0:T(8,128)(2,1)S(1)}, bf16[128,2304]{1,0:T(8...) custom-call(s32[4,8]{1,0:T(4,128)S(1)} %get-tuple-element.19.clips, ...), custom_call_target="tpu_custom_call" | custom-call | tf_op jit(solution)/shard_map/pallas_call | solution.py:349
  63.3 13.3 %all_to_all.15 = bf16[8,16,2304]{2,1,0:T(8,128)(2,1)S(1)} all-to-all(bf16[8,16,2304]{2,1,0:T(8,128)(2,1)S(1)} %bitcast.9), channel_id=1, replica_groups={{0,1,2,3,4,5,6,7},{8,9,10,11,12,13,14,15},{16,17,18,19,20,21,22,23},{24..., dimensions={0} | all-to-all | bytes 1179648 | tf_op jit(solution)/shard_map/all_to_all | solution.py:512
  76.6 2.0 %shard_map.141 = bf16[128,2304]{1,0:T(8,128)(2,1)S(1)} custom-call(s32[4,8]{1,0:T(4,128)S(1)} %get-tuple-element.19.clips, bf16[128,2304]{1,0:T(8,128)(2,1)S(1)} %bitcast.7), custom_call_target="tpu_custom_call" | custom-call | tf_op jit(solution)/shard_map/pallas_call | solution.py:349
  78.6 12.8 %all_to_all.16 = bf16[8,16,2304]{2,1,0:T(8,128)(2,1)S(1)} all-to-all(bf16[8,16,2304]{2,1,0:T(8,128)(2,1)S(1)} %bitcast.8), channel_id=1, replica_groups={{0,1,2,3,4,5,6,7},{8,9,10,11,12,13,14,15},{16,17,18,19,20,21,22,23},{24..., dimensions={0} | all-to-all | bytes 1179648 | tf_op jit(solution)/shard_map/all_to_all | solution.py:512
  91.3 5.7 %shard_map.142 = (bf16[128,1152]{1,0:T(8,128)(2,1)}, bf16[128,1152]{1,0:T(8,128)(2,1)}, bf16[32,2,1152]{2,1,0:T(2,128)(2,1)S(1)}) custom-call(s32[4,8]{1,0:T(4,128)S(1)} %get-tuple-element.19.clips, bf16[128,2304]{1,0:T(8,128)(2,1)S(1)} %bitcast.6, bf16[2,128,1152]{2,1,0:T(8,128)(2,1)S(1)} %get-tuple-element.20.tokens, ...), custom_call_target="tpu_custom_call" | custom-call | tf_op jit(solution)/shard_map/pallas_call | solution.py:349
  97.1 11.7 %all_to_all.17 = bf16[32,2,1152]{2,1,0:T(2,128)(2,1)S(1)} all-to-all(bf16[32,2,1152]{2,1,0:T(2,128)(2,1)S(1)} %get-tuple-element.34), channel_id=1, replica_groups=mesh['dp'=2,'ctx'=16] {'dp','ctx'}, dimensions={0} | all-to-all | bytes 294912 | tf_op jit(solution)/shard_map/all_to_all | solution.py:556
  (43 shorter events, 4.3 us)
Async XLA Ops:
  2.0 8.1 %collective-permute-start.5 = (bf16[144,1152]{1,0:T(8,128)(2,1)S(1)}, bf16[144,1152]{1,0:T(8,128)(2,1)S(1)}, u32[]{:S(2)}, u32[]{:S(2)}) collective-permute-start(bf16[144,1152]{1,0:T(8,128)(2,1)S(1)} %get-tuple-element.36.refs_0_), channel_id=1, source_target_pairs={{0,4},{1,3},{4,8},{5,1},{8,12},{9,5},{12,14},{13,9},{14,10},{15,13... | collective-permute-start | bytes 995336 | tf_op jit(solution)/shard_map/ppermute | solution.py:376
  5.0 8.8 %collective-permute-start = (bf16[144,1152]{1,0:T(8,128)(2,1)S(1)}, bf16[144,1152]{1,0:T(8,128)(2,1)S(1)}, u32[]{:S(2)}, u32[]{:S(2)}) collective-permute-start(bf16[144,1152]{1,0:T(8,128)(2,1)S(1)} %get-tuple-element.36.refs_0_), channel_id=1, source_target_pairs={{0,1},{1,0},{2,3},{3,2},{4,5},{5,4},{6,7},{7,6},{8,9},{9,8},{10,11... | collective-permute-start | bytes 995336 | tf_op jit(solution)/shard_map/ppermute | solution.py:382
  10.1 9.0 %collective-permute-start.16 = (bf16[144,1152]{1,0:T(8,128)(2,1)S(1)}, bf16[144,1152]{1,0:T(8,128)(2,1)S(1)}, u32[]{:S(2)}, u32[]{:S(2)}) collective-permute-start(bf16[144,1152]{1,0:T(8,128)(2,1)S(1)} %collective-permute-done.5.refs_2_), channel_id=1, source_target_pairs={{0,16},{16,0},{1,17},{17,1},{2,18},{18,2},{3,19},{19,3},{4,20},{20... | collective-permute-start | bytes 995336 | tf_op jit(solution)/shard_map/ppermute | solution.py:379
  12.1 7.0 %collective-permute-start.4 = (bf16[144,1152]{1,0:T(8,128)(2,1)S(1)}, bf16[144,1152]{1,0:T(8,128)(2,1)S(1)}, u32[]{:S(2)}, u32[]{:S(2)}) collective-permute-start(bf16[144,1152]{1,0:T(8,128)(2,1)S(1)} %get-tuple-element.35.refs_16_), channel_id=1, source_target_pairs={{0,1},{1,0},{2,3},{3,2},{4,5},{5,4},{6,7},{7,6},{8,9},{9,8},{10,11... | collective-permute-start | bytes 995336 | tf_op jit(solution)/shard_map/ppermute | solution.py:382
  12.1 8.8 %collective-permute-start.7 = (bf16[144,1152]{1,0:T(8,128)(2,1)S(1)}, bf16[144,1152]{1,0:T(8,128)(2,1)S(1)}, u32[]{:S(2)}, u32[]{:S(2)}) collective-permute-start(bf16[144,1152]{1,0:T(8,128)(2,1)S(1)} %collective-permute-done.5.refs_2_), channel_id=1, source_target_pairs={{0,4},{1,3},{4,8},{5,1},{8,12},{9,5},{12,14},{13,9},{14,10},{15,13... | collective-permute-start | bytes 995336 | tf_op jit(solution)/shard_map/ppermute | solution.py:376
  13.6 7.4 %collective-permute-start.6 = (bf16[144,1152]{1,0:T(8,128)(2,1)S(1)}, bf16[144,1152]{1,0:T(8,128)(2,1)S(1)}, u32[]{:S(2)}, u32[]{:S(2)}) collective-permute-start(bf16[144,1152]{1,0:T(8,128)(2,1)S(1)} %collective-permute-done.5.refs_2_), channel_id=1, source_target_pairs={{0,1},{1,0},{2,3},{3,2},{4,5},{5,4},{6,7},{7,6},{8,9},{9,8},{10,11... | collective-permute-start | bytes 995336 | tf_op jit(solution)/shard_map/ppermute | solution.py:382
  13.8 8.9 %collective-permute-start.1 = (bf16[144,1152]{1,0:T(8,128)(2,1)S(1)}, bf16[144,1152]{1,0:T(8,128)(2,1)S(1)}, u32[]{:S(2)}, u32[]{:S(2)}) collective-permute-start(bf16[144,1152]{1,0:T(8,128)(2,1)S(1)} %collective-permute-done.refs_1_), channel_id=1, source_target_pairs={{0,4},{1,3},{4,8},{5,1},{8,12},{9,5},{12,14},{13,9},{14,10},{15,13... | collective-permute-start | bytes 995336 | tf_op jit(solution)/shard_map/ppermute | solution.py:376
  19.1 4.9 %collective-permute-start.23 = (bf16[144,1152]{1,0:T(8,128)(2,1)S(1)}, bf16[144,1152]{1,0:T(8,128)(2,1)S(1)}, u32[]{:S(2)}, u32[]{:S(2)}) collective-permute-start(bf16[144,1152]{1,0:T(8,128)(2,1)S(1)} %collective-permute-done.16.refs_18_), channel_id=1, source_target_pairs={{0,1},{1,0},{2,3},{3,2},{4,5},{5,4},{6,7},{7,6},{8,9},{9,8},{10,11... | collective-permute-start | bytes 995336 | tf_op jit(solution)/shard_map/ppermute | solution.py:382
  19.1 7.2 %collective-permute-start.17 = (bf16[144,1152]{1,0:T(8,128)(2,1)S(1)}, bf16[144,1152]{1,0:T(8,128)(2,1)S(1)}, u32[]{:S(2)}, u32[]{:S(2)}) collective-permute-start(bf16[144,1152]{1,0:T(8,128)(2,1)S(1)} %collective-permute-done.16.refs_18_), channel_id=1, source_target_pairs={{0,4},{1,3},{4,8},{5,1},{8,12},{9,5},{12,14},{13,9},{14,10},{15,13... | collective-permute-start | bytes 995336 | tf_op jit(solution)/shard_map/ppermute | solution.py:376
  20.8 7.1 %collective-permute-start.11 = (bf16[144,1152]{1,0:T(8,128)(2,1)S(1)}, bf16[144,1152]{1,0:T(8,128)(2,1)S(1)}, u32[]{:S(2)}, u32[]{:S(2)}) collective-permute-start(bf16[144,1152]{1,0:T(8,128)(2,1)S(1)} %collective-permute-done.7.refs_3_), channel_id=1, source_target_pairs={{0,1},{1,0},{2,3},{3,2},{4,5},{5,4},{6,7},{7,6},{8,9},{9,8},{10,11... | collective-permute-start | bytes 995336 | tf_op jit(solution)/shard_map/ppermute | solution.py:382
  21.0 8.8 %collective-permute-start.8 = (bf16[144,1152]{1,0:T(8,128)(2,1)S(1)}, bf16[144,1152]{1,0:T(8,128)(2,1)S(1)}, u32[]{:S(2)}, u32[]{:S(2)}) collective-permute-start(bf16[144,1152]{1,0:T(8,128)(2,1)S(1)} %collective-permute-done.7.refs_3_), channel_id=1, source_target_pairs={{0,4},{1,3},{4,8},{5,1},{8,12},{9,5},{12,14},{13,9},{14,10},{15,13... | collective-permute-start | bytes 995336 | tf_op jit(solution)/shard_map/ppermute | solution.py:376
  22.7 9.4 %collective-permute-start.20 = (bf16[144,1152]{1,0:T(8,128)(2,1)S(1)}, bf16[144,1152]{1,0:T(8,128)(2,1)S(1)}, u32[]{:S(2)}, u32[]{:S(2)}) collective-permute-start(bf16[144,1152]{1,0:T(8,128)(2,1)S(1)} %collective-permute-done.1.refs_6_), channel_id=1, source_target_pairs={{0,16},{16,0},{1,17},{17,1},{2,18},{18,2},{3,19},{19,3},{4,20},{20... | collective-permute-start | bytes 995336 | tf_op jit(solution)/shard_map/ppermute | solution.py:379
  24.0 8.1 %collective-permute-start.3 = (bf16[144,1152]{1,0:T(8,128)(2,1)S(1)}, bf16[144,1152]{1,0:T(8,128)(2,1)S(1)}, u32[]{:S(2)}, u32[]{:S(2)}) collective-permute-start(bf16[144,1152]{1,0:T(8,128)(2,1)S(1)} %collective-permute-done.1.refs_6_), channel_id=1, source_target_pairs={{0,1},{1,0},{2,3},{3,2},{4,5},{5,4},{6,7},{7,6},{8,9},{9,8},{10,11... | collective-permute-start | bytes 995336 | tf_op jit(solution)/shard_map/ppermute | solution.py:382
  26.3 7.4 %collective-permute-start.2 = (bf16[144,1152]{1,0:T(8,128)(2,1)S(1)}, bf16[144,1152]{1,0:T(8,128)(2,1)S(1)}, u32[]{:S(2)}, u32[]{:S(2)}) collective-permute-start(bf16[144,1152]{1,0:T(8,128)(2,1)S(1)} %collective-permute-done.1.refs_6_), channel_id=1, source_target_pairs={{0,4},{1,3},{4,8},{5,1},{8,12},{9,5},{12,14},{13,9},{14,10},{15,13... | collective-permute-start | bytes 995336 | tf_op jit(solution)/shard_map/ppermute | solution.py:376
  28.0 5.9 %collective-permute-start.24 = (bf16[144,1152]{1,0:T(8,128)(2,1)S(1)}, bf16[144,1152]{1,0:T(8,128)(2,1)S(1)}, u32[]{:S(2)}, u32[]{:S(2)}) collective-permute-start(bf16[144,1152]{1,0:T(8,128)(2,1)S(1)} %collective-permute-done.17.refs_19_), channel_id=1, source_target_pairs={{0,1},{1,0},{2,3},{3,2},{4,5},{5,4},{6,7},{7,6},{8,9},{9,8},{10,11... | collective-permute-start | bytes 995336 | tf_op jit(solution)/shard_map/ppermute | solution.py:382
  29.8 9.8 %collective-permute-start.18 = (bf16[144,1152]{1,0:T(8,128)(2,1)S(1)}, bf16[144,1152]{1,0:T(8,128)(2,1)S(1)}, u32[]{:S(2)}, u32[]{:S(2)}) collective-permute-start(bf16[144,1152]{1,0:T(8,128)(2,1)S(1)} %collective-permute-done.8.refs_4_), channel_id=1, source_target_pairs={{0,16},{16,0},{1,17},{17,1},{2,18},{18,2},{3,19},{19,3},{4,20},{20... | collective-permute-start | bytes 995336 | tf_op jit(solution)/shard_map/ppermute | solution.py:379
  32.1 7.6 %collective-permute-start.12 = (bf16[144,1152]{1,0:T(8,128)(2,1)S(1)}, bf16[144,1152]{1,0:T(8,128)(2,1)S(1)}, u32[]{:S(2)}, u32[]{:S(2)}) collective-permute-start(bf16[144,1152]{1,0:T(8,128)(2,1)S(1)} %collective-permute-done.8.refs_4_), channel_id=1, source_target_pairs={{0,1},{1,0},{2,3},{3,2},{4,5},{5,4},{6,7},{7,6},{8,9},{9,8},{10,11... | collective-permute-start | bytes 995336 | tf_op jit(solution)/shard_map/ppermute | solution.py:382
  32.1 9.2 %collective-permute-start.9 = (bf16[144,1152]{1,0:T(8,128)(2,1)S(1)}, bf16[144,1152]{1,0:T(8,128)(2,1)S(1)}, u32[]{:S(2)}, u32[]{:S(2)}) collective-permute-start(bf16[144,1152]{1,0:T(8,128)(2,1)S(1)} %collective-permute-done.8.refs_4_), channel_id=1, source_target_pairs={{0,4},{1,3},{4,8},{5,1},{8,12},{9,5},{12,14},{13,9},{14,10},{15,13... | collective-permute-start | bytes 995336 | tf_op jit(solution)/shard_map/ppermute | solution.py:376
  33.7 7.6 %collective-permute-start.27 = (bf16[144,1152]{1,0:T(8,128)(2,1)S(1)}, bf16[144,1152]{1,0:T(8,128)(2,1)S(1)}, u32[]{:S(2)}, u32[]{:S(2)}) collective-permute-start(bf16[144,1152]{1,0:T(8,128)(2,1)S(1)} %collective-permute-done.20.refs_22_), channel_id=1, source_target_pairs={{0,1},{1,0},{2,3},{3,2},{4,5},{5,4},{6,7},{7,6},{8,9},{9,8},{10,11... | collective-permute-start | bytes 995336 | tf_op jit(solution)/shard_map/ppermute | solution.py:382
  33.9 8.9 %collective-permute-start.21 = (bf16[144,1152]{1,0:T(8,128)(2,1)S(1)}, bf16[144,1152]{1,0:T(8,128)(2,1)S(1)}, u32[]{:S(2)}, u32[]{:S(2)}) collective-permute-start(bf16[144,1152]{1,0:T(8,128)(2,1)S(1)} %collective-permute-done.20.refs_22_), channel_id=1, source_target_pairs={{0,4},{1,3},{4,8},{5,1},{8,12},{9,5},{12,14},{13,9},{14,10},{15,13... | collective-permute-start | bytes 995336 | tf_op jit(solution)/shard_map/ppermute | solution.py:376
  39.7 4.7 %collective-permute-start.14 = (bf16[144,1152]{1,0:T(8,128)(2,1)S(1)}, bf16[144,1152]{1,0:T(8,128)(2,1)S(1)}, u32[]{:S(2)}, u32[]{:S(2)}) collective-permute-start(bf16[144,1152]{1,0:T(8,128)(2,1)S(1)} %get-tuple-element.22.refs_7_), channel_id=1, source_target_pairs={{0,1},{1,0},{2,3},{3,2},{4,5},{5,4},{6,7},{7,6},{8,9},{9,8},{10,11... | collective-permute-start | bytes 995336 | tf_op jit(solution)/shard_map/ppermute | solution.py:382
  39.7 7.1 %collective-permute-start.10 = (bf16[144,1152]{1,0:T(8,128)(2,1)S(1)}, bf16[144,1152]{1,0:T(8,128)(2,1)S(1)}, u32[]{:S(2)}, u32[]{:S(2)}) collective-permute-start(bf16[144,1152]{1,0:T(8,128)(2,1)S(1)} %get-tuple-element.22.refs_7_), channel_id=1, source_target_pairs={{0,4},{1,3},{4,8},{5,1},{8,12},{9,5},{12,14},{13,9},{14,10},{15,13... | collective-permute-start | bytes 995336 | tf_op jit(solution)/shard_map/ppermute | solution.py:376
  41.3 5.5 %collective-permute-start.25 = (bf16[144,1152]{1,0:T(8,128)(2,1)S(1)}, bf16[144,1152]{1,0:T(8,128)(2,1)S(1)}, u32[]{:S(2)}, u32[]{:S(2)}) collective-permute-start(bf16[144,1152]{1,0:T(8,128)(2,1)S(1)} %collective-permute-done.18.refs_20_), channel_id=1, source_target_pairs={{0,1},{1,0},{2,3},{3,2},{4,5},{5,4},{6,7},{7,6},{8,9},{9,8},{10,11... | collective-permute-start | bytes 995336 | tf_op jit(solution)/shard_map/ppermute | solution.py:382
  41.3 10.2 %collective-permute-start.19 = (bf16[144,1152]{1,0:T(8,128)(2,1)S(1)}, bf16[144,1152]{1,0:T(8,128)(2,1)S(1)}, u32[]{:S(2)}, u32[]{:S(2)}) collective-permute-start(bf16[144,1152]{1,0:T(8,128)(2,1)S(1)} %collective-permute-done.9.refs_5_), channel_id=1, source_target_pairs={{0,16},{16,0},{1,17},{17,1},{2,18},{18,2},{3,19},{19,3},{4,20},{20... | collective-permute-start | bytes 995336 | tf_op jit(solution)/shard_map/ppermute | solution.py:379
  42.8 8.7 %collective-permute-start.22 = (bf16[144,1152]{1,0:T(8,128)(2,1)S(1)}, bf16[144,1152]{1,0:T(8,128)(2,1)S(1)}, u32[]{:S(2)}, u32[]{:S(2)}) collective-permute-start(bf16[144,1152]{1,0:T(8,128)(2,1)S(1)} %collective-permute-done.21.refs_23_), channel_id=1, source_target_pairs={{0,4},{1,3},{4,8},{5,1},{8,12},{9,5},{12,14},{13,9},{14,10},{15,13... | collective-permute-start | bytes 995336 | tf_op jit(solution)/shard_map/ppermute | solution.py:376
  44.4 7.6 %collective-permute-start.13 = (bf16[144,1152]{1,0:T(8,128)(2,1)S(1)}, bf16[144,1152]{1,0:T(8,128)(2,1)S(1)}, u32[]{:S(2)}, u32[]{:S(2)}) collective-permute-start(bf16[144,1152]{1,0:T(8,128)(2,1)S(1)} %collective-permute-done.9.refs_5_), channel_id=1, source_target_pairs={{0,1},{1,0},{2,3},{3,2},{4,5},{5,4},{6,7},{7,6},{8,9},{9,8},{10,11... | collective-permute-start | bytes 995336 | tf_op jit(solution)/shard_map/ppermute | solution.py:382
  46.8 5.2 %collective-permute-start.28 = (bf16[144,1152]{1,0:T(8,128)(2,1)S(1)}, bf16[144,1152]{1,0:T(8,128)(2,1)S(1)}, u32[]{:S(2)}, u32[]{:S(2)}) collective-permute-start(bf16[144,1152]{1,0:T(8,128)(2,1)S(1)} %collective-permute-done.21.refs_23_), channel_id=1, source_target_pairs={{0,1},{1,0},{2,3},{3,2},{4,5},{5,4},{6,7},{7,6},{8,9},{9,8},{10,11... | collective-permute-start | bytes 995336 | tf_op jit(solution)/shard_map/ppermute | solution.py:382
  46.8 5.2 %collective-permute-start.15 = (bf16[144,1152]{1,0:T(8,128)(2,1)S(1)}, bf16[144,1152]{1,0:T(8,128)(2,1)S(1)}, u32[]{:S(2)}, u32[]{:S(2)}) collective-permute-start(bf16[144,1152]{1,0:T(8,128)(2,1)S(1)} %collective-permute-done.10.refs_8_), channel_id=1, source_target_pairs={{0,1},{1,0},{2,3},{3,2},{4,5},{5,4},{6,7},{7,6},{8,9},{9,8},{10,11... | collective-permute-start | bytes 995336 | tf_op jit(solution)/shard_map/ppermute | solution.py:382
  51.5 1.6 %collective-permute-start.26 = (bf16[144,1152]{1,0:T(8,128)(2,1)S(1)}, bf16[144,1152]{1,0:T(8,128)(2,1)S(1)}, u32[]{:S(2)}, u32[]{:S(2)}) collective-permute-start(bf16[144,1152]{1,0:T(8,128)(2,1)S(1)} %collective-permute-done.19.refs_21_), channel_id=1, source_target_pairs={{0,1},{1,0},{2,3},{3,2},{4,5},{5,4},{6,7},{7,6},{8,9},{9,8},{10,11... | collective-permute-start | bytes 995336 | tf_op jit(solution)/shard_map/ppermute | solution.py:382
  51.5 2.1 %collective-permute-start.29 = (bf16[144,1152]{1,0:T(8,128)(2,1)S(1)}, bf16[144,1152]{1,0:T(8,128)(2,1)S(1)}, u32[]{:S(2)}, u32[]{:S(2)}) collective-permute-start(bf16[144,1152]{1,0:T(8,128)(2,1)S(1)} %collective-permute-done.22.refs_24_), channel_id=1, source_target_pairs={{0,1},{1,0},{2,3},{3,2},{4,5},{5,4},{6,7},{7,6},{8,9},{9,8},{10,11... | collective-permute-start | bytes 995336 | tf_op jit(solution)/shard_map/ppermute | solution.py:382
